TPU v7x, 32 devices: a whole 2x2x4 slice. The times are simulated.
32 devices in a mesh: dp: 4 (over y, x), wide: 8 (over z, core).
Axes of the slice: x: 2, y: 2, z: 4, core: 2. Of those that a mesh axis runs over, the one named last changes fastest.
Arguments:
- doc_tokens: bfloat16 [2, 32, 512, 768], P(None, ('dp', 'wide')), may hold values from -6 to 6
- query_tokens: bfloat16 [2, 64, 32, 768], P(None, ('dp', 'wide')), may hold values from -6 to 6
- query_lengths: int32 [2, 64], P(None, ('dp', 'wide')), may hold values from 8 to 32
- retrieved: int32 [2, 64, 32, 32], P(None, ('dp', 'wide')), may hold values from 0 to 4095
- targets: int32 [2, 64], P(None, ('dp', 'wide')), may hold values from 0 to 7
- q_weight: bfloat16 [768, 768], P(('dp', 'wide')), may hold values from -0.02734375 to 0.02734375
- k_weight: bfloat16 [768, 768], P(('dp', 'wide')), may hold values from -0.21875 to 0.21875
- v_weight: bfloat16 [768, 768], P(('dp', 'wide')), may hold values from -0.21875 to 0.21875
- o_weight: bfloat16 [768, 768], P(('dp', 'wide')), may hold values from -1.25 to 1.25
- gate_weight: bfloat16 [768, 2048], P(('dp', 'wide')), may hold values from -0.21875 to 0.21875
- up_weight: bfloat16 [768, 2048], P(('dp', 'wide')), may hold values from -0.21875 to 0.21875
- down_weight: bfloat16 [2048, 768], P(('dp', 'wide')), may hold values from -0.21875 to 0.21875
- proj_weight: bfloat16 [768, 128], P(('dp', 'wide')), may hold values from -0.21875 to 0.21875
- attn_gain: bfloat16 [768], P(('dp', 'wide')), may hold values from 0.5 to 1.5
- ffn_gain: bfloat16 [768], P(('dp', 'wide')), may hold values from 0.5 to 1.5
- final_gain: bfloat16 [768], P(('dp', 'wide')), may hold values from 0.5 to 1.5
- rel_bias: bfloat16 [32, 12], replicated, may hold values from -4 to 4
Outputs:
- losses: float32 [2, 64], P(None, ('dp', 'wide'))
- doc_grad: float32 [2, 32, 512, 768], P(None, ('dp', 'wide'))
- query_grad: float32 [2, 64, 32, 768], P(None, ('dp', 'wide'))
- q_grad: float32 [768, 768], P(('dp', 'wide'))
- k_grad: float32 [768, 768], P(('dp', 'wide'))
- v_grad: float32 [768, 768], P(('dp', 'wide'))
- o_grad: float32 [768, 768], P(('dp', 'wide'))
- gate_grad: float32 [768, 2048], P(('dp', 'wide'))
- up_grad: float32 [768, 2048], P(('dp', 'wide'))
- down_grad: float32 [2048, 768], P(('dp', 'wide'))
- proj_grad: float32 [768, 128], P(('dp', 'wide'))
- attn_gain_grad: float32 [768], P(('dp', 'wide'))
- ffn_gain_grad: float32 [768], P(('dp', 'wide'))
- final_gain_grad: float32 [768], P(('dp', 'wide'))
- bias_grad: float32 [32, 12], replicated
Inputs may be any that keep to these rules, and one draw needn't show every extreme that they name: `retrieved`: each entry names a token of a document of the same micro-batch and group: document w, token t as w * 512 + t; entries may repeat. `targets`: the positive document's number within the group.
All inputs are finite; a program needn't handle non-finite values.
Results may differ from a plain program's by a relative error of at most 0.023.
Values may be sent and summed in bfloat16 or wider, within the bound.
A program may use at most 256 MiB of HBM per device.

v0:
```python
import jax
import jax.numpy as jnp
from jax import lax
from jax.sharding import PartitionSpec as P

eps_norm = 1e-06
score_scale = 6.0
mask_fill = -1000000000.0
top_precision = lax.Precision.HIGHEST
block_rows = 512


def cut_along(x, dim, length):
    shape = x.shape
    tiles = x.reshape(*shape[:dim], length, shape[dim] // length, *shape[dim + 1 :])
    return jnp.moveaxis(tiles, dim, 0)


def sent_and_summed(x, axis, dim):
    length = lax.axis_size(axis)
    tiles = lax.all_to_all(cut_along(x, dim, length), axis, 0, 0, tiled=True)
    return jnp.sum(tiles.astype(jnp.float32), axis=0)


def contract_rows(left_mat, right_mat):
    return lax.dot_general(
        left_mat, right_mat, (((0,), (0,)), ((), ())), preferred_element_type=jnp.float32
    )


def contract_cols(left_mat, right_mat):
    return lax.dot_general(
        left_mat, right_mat, (((1,), (1,)), ((), ())), preferred_element_type=jnp.float32
    )


def matmul(left_mat, right_mat):
    return jnp.dot(left_mat, right_mat, preferred_element_type=jnp.float32)


def rms_forward(values, gain_vec):
    inverse = lax.rsqrt(jnp.mean(values * values, axis=-1, keepdims=True) + eps_norm)
    return (values * inverse * gain_vec, inverse)


def rms_backward(values, inverse, gain_vec, upstream):
    scaled = upstream * gain_vec
    gain_grad = jnp.sum(upstream * values * inverse, axis=0)
    inner_mean = jnp.mean(scaled * values, axis=-1, keepdims=True)
    return (inverse * scaled - values * inverse * inverse * inverse * inner_mean, gain_grad)


def bucket_onehot(length, bucket_count):
    places = jnp.arange(length, dtype=jnp.int32)
    offset_ij = places[None, :] - places[:, None]
    distance = jnp.abs(offset_ij)
    steps_far = jnp.zeros_like(distance)
    for power_step in range(1, 8):
        steps_far = steps_far + (distance * distance >= 64 * 2**power_step).astype(jnp.int32)
    bucket_ids = jnp.where(offset_ij > 0, 16, 0) + jnp.where(distance < 8, distance, 8 + steps_far)
    return (
        bucket_ids[:, :, None] == jnp.arange(bucket_count, dtype=jnp.int32)[None, None, :]
    ).astype(jnp.float32)


def attention_scores(queries_h, keys_h, bias_full, valid_keys):
    scores = (
        jnp.einsum("bqhd,bkhd->bhqk", queries_h, keys_h, preferred_element_type=jnp.float32)
        + bias_full[None]
    )
    return jnp.where(valid_keys[:, None, None, :], scores, mask_fill)


def encode_forward(tokens, valid_keys, bias_full, full_weights):
    (
        w_query,
        w_key,
        w_value,
        w_out,
        w_gate,
        w_up,
        w_down,
        w_proj,
        gain_attn,
        gain_ffn,
        gain_final,
    ) = full_weights
    batch_size, length, width_size = tokens.shape
    head_count = bias_full.shape[0]
    flat_rows = tokens.astype(jnp.float32).reshape(batch_size * length, width_size)
    normed_full, inverse_one = rms_forward(flat_rows, gain_attn.astype(jnp.float32))
    normed = normed_full.astype(jnp.bfloat16)

    def split_heads(weight):
        return (
            matmul(normed, weight).astype(jnp.bfloat16).reshape(batch_size, length, head_count, -1)
        )

    queries_h = split_heads(w_query)
    keys_h = split_heads(w_key)
    values_h = split_heads(w_value)
    scores = attention_scores(queries_h, keys_h, bias_full, valid_keys)
    row_top = jnp.max(scores, axis=-1, keepdims=True)
    shifted = jnp.exp(scores - row_top)
    row_totals = jnp.sum(shifted, axis=-1, keepdims=True)
    probs_attn = shifted / row_totals
    log_total = row_top + jnp.log(row_totals)
    context = jnp.einsum(
        "bhqk,bkhd->bqhd",
        probs_attn.astype(jnp.bfloat16),
        values_h,
        preferred_element_type=jnp.float32,
    )
    context = context.astype(jnp.bfloat16).reshape(batch_size * length, width_size)
    hidden = flat_rows + matmul(context, w_out)
    normed_two_full, inverse_two = rms_forward(hidden, gain_ffn.astype(jnp.float32))
    normed_two = normed_two_full.astype(jnp.bfloat16)
    gate_pre = matmul(normed_two, w_gate)
    up_pre = matmul(normed_two, w_up)
    activated = (jax.nn.gelu(gate_pre) * up_pre).astype(jnp.bfloat16)
    layer_out = hidden + matmul(activated, w_down)
    normed_end_full, inverse_end = rms_forward(layer_out, gain_final.astype(jnp.float32))
    normed_end = normed_end_full.astype(jnp.bfloat16)
    embedded = matmul(normed_end, w_proj).astype(jnp.bfloat16)
    kept_state = (
        flat_rows,
        inverse_one,
        normed,
        queries_h,
        keys_h,
        values_h,
        log_total,
        context,
        hidden,
        inverse_two,
        normed_two,
        gate_pre,
        up_pre,
        activated,
        layer_out,
        inverse_end,
        normed_end,
    )
    return (embedded, kept_state)


def encode_backward(grad_emb, kept_state, valid_keys, bias_full, onehot_table, full_weights):
    (
        w_query,
        w_key,
        w_value,
        w_out,
        w_gate,
        w_up,
        w_down,
        w_proj,
        gain_attn,
        gain_ffn,
        gain_final,
    ) = full_weights
    (
        flat_rows,
        inverse_one,
        normed,
        queries_h,
        keys_h,
        values_h,
        log_total,
        context,
        hidden,
        inverse_two,
        normed_two,
        gate_pre,
        up_pre,
        activated,
        layer_out,
        inverse_end,
        normed_end,
    ) = kept_state
    row_count, width_size = flat_rows.shape
    grad_low = grad_emb.astype(jnp.bfloat16)
    proj_grad = contract_rows(normed_end, grad_low)
    d_normed_end = contract_cols(grad_low, w_proj)
    d_layer, final_gain_grad = rms_backward(
        layer_out, inverse_end, gain_final.astype(jnp.float32), d_normed_end
    )
    d_layer_low = d_layer.astype(jnp.bfloat16)
    down_grad = contract_rows(activated, d_layer_low)
    d_activated = contract_cols(d_layer_low, w_down)
    unused_value, pull_back = jax.vjp(
        lambda first_arg, second_arg: jax.nn.gelu(first_arg) * second_arg, gate_pre, up_pre
    )
    d_gate, d_up = pull_back(d_activated)
    d_gate = d_gate.astype(jnp.bfloat16)
    d_up = d_up.astype(jnp.bfloat16)
    gate_grad = contract_rows(normed_two, d_gate)
    up_grad = contract_rows(normed_two, d_up)
    d_normed_two = contract_cols(d_gate, w_gate) + contract_cols(d_up, w_up)
    d_hidden_norm, ffn_gain_grad = rms_backward(
        hidden, inverse_two, gain_ffn.astype(jnp.float32), d_normed_two
    )
    d_hidden = d_layer + d_hidden_norm
    d_hidden_low = d_hidden.astype(jnp.bfloat16)
    out_grad = contract_rows(context, d_hidden_low)
    d_context = contract_cols(d_hidden_low, w_out).astype(jnp.bfloat16).reshape(queries_h.shape)
    scores = attention_scores(queries_h, keys_h, bias_full, valid_keys)
    probs_attn = jnp.exp(scores - log_total)
    d_probs = jnp.einsum("bqhd,bkhd->bhqk", d_context, values_h, preferred_element_type=jnp.float32)
    d_values = jnp.einsum(
        "bhqk,bqhd->bkhd",
        probs_attn.astype(jnp.bfloat16),
        d_context,
        preferred_element_type=jnp.float32,
    )
    d_values = d_values.astype(jnp.bfloat16).reshape(row_count, width_size)
    d_scores = probs_attn * (d_probs - jnp.sum(probs_attn * d_probs, axis=-1, keepdims=True))
    table_grad = jnp.einsum(
        "hij,ijb->bh", jnp.sum(d_scores, axis=0), onehot_table, precision=top_precision
    )
    d_scores_low = d_scores.astype(jnp.bfloat16)
    d_queries = jnp.einsum(
        "bhqk,bkhd->bqhd", d_scores_low, keys_h, preferred_element_type=jnp.float32
    )
    d_queries = d_queries.astype(jnp.bfloat16).reshape(row_count, width_size)
    d_keys = jnp.einsum(
        "bhqk,bqhd->bkhd", d_scores_low, queries_h, preferred_element_type=jnp.float32
    )
    d_keys = d_keys.astype(jnp.bfloat16).reshape(row_count, width_size)
    query_w_grad = contract_rows(normed, d_queries)
    key_w_grad = contract_rows(normed, d_keys)
    value_w_grad = contract_rows(normed, d_values)
    d_normed = (
        contract_cols(d_queries, w_query)
        + contract_cols(d_keys, w_key)
        + contract_cols(d_values, w_value)
    )
    d_flat, attn_gain_grad = rms_backward(
        flat_rows, inverse_one, gain_attn.astype(jnp.float32), d_normed
    )
    grad_list = (
        query_w_grad,
        key_w_grad,
        value_w_grad,
        out_grad,
        gate_grad,
        up_grad,
        down_grad,
        proj_grad,
        attn_gain_grad,
        ffn_gain_grad,
        final_gain_grad,
    )
    return (d_hidden + d_flat, grad_list, table_grad)


def pool_rows(row_block, picks_block, doc_emb, positions):
    scores_raw = contract_cols(row_block, doc_emb) * doc_emb.shape[1] ** (-0.5)
    multiple = jnp.sum(
        (picks_block[:, :, None] == positions[None, None, :]).astype(jnp.float32), axis=1
    )
    present = jnp.sum(multiple, axis=-1)
    totals_sum = jnp.sum(multiple * jnp.exp(scores_raw), axis=-1) + (present == 0).astype(
        jnp.float32
    )
    return (scores_raw, multiple, totals_sum)


def score_forward(query_all, picks_all, doc_emb, positions):
    row_count = query_all.shape[0]
    block_size = min(block_rows, row_count)
    block_count = row_count // block_size

    def one_block(bundle):
        scores_raw, multiple, totals_sum = pool_rows(bundle[0], bundle[1], doc_emb, positions)
        return jnp.log(totals_sum)

    pooled = lax.map(
        one_block,
        (
            query_all.reshape(block_count, block_size, -1),
            picks_all.reshape(block_count, block_size, -1),
        ),
    )
    return pooled.reshape(row_count)


def score_backward(query_all, picks_all, doc_emb, positions, pooled_grad):
    row_count = query_all.shape[0]
    block_size = min(block_rows, row_count)
    block_count = row_count // block_size
    scale_factor = doc_emb.shape[1] ** (-0.5)

    def one_block(doc_acc, bundle):
        row_block, picks_block, grad_block = bundle
        scores_raw, multiple, totals_sum = pool_rows(row_block, picks_block, doc_emb, positions)
        d_raw = (grad_block / totals_sum)[:, None] * multiple * jnp.exp(scores_raw) * scale_factor
        d_low = d_raw.astype(jnp.bfloat16)
        return (doc_acc + contract_rows(d_low, row_block), matmul(d_low, doc_emb))

    start_acc = jnp.zeros(doc_emb.shape, jnp.float32)
    doc_grad, query_blocks = lax.scan(
        one_block,
        start_acc,
        (
            query_all.reshape(block_count, block_size, -1),
            picks_all.reshape(block_count, block_size, -1),
            pooled_grad.reshape(block_count, block_size),
        ),
    )
    return (doc_grad, query_blocks.reshape(row_count, -1))


def query_loss(pooled_query, own_picks, lengths, goal_ids, doc_len):
    wide_count, token_count = pooled_query.shape
    query_count = lengths.shape[0]
    slot_count = token_count // query_count
    owner_doc = own_picks // doc_len
    doc_ids = jnp.arange(wide_count, dtype=jnp.int32)
    hit_mask = jnp.any(owner_doc[None, :, :] == doc_ids[:, None, None], axis=-1).astype(jnp.float32)
    valid_mask = (
        (jnp.arange(slot_count, dtype=jnp.int32)[None, :] < lengths[:, None])
        .astype(jnp.float32)
        .reshape(token_count)
    )
    counts = jnp.sum((hit_mask * valid_mask).reshape(wide_count, query_count, slot_count), axis=-1)
    divisor = jnp.maximum(counts, 1.0)
    summed = jnp.sum(
        (pooled_query * valid_mask).reshape(wide_count, query_count, slot_count), axis=-1
    )
    logits = score_scale * summed / divisor
    col_top = jnp.max(logits, axis=0, keepdims=True)
    shifted = jnp.exp(logits - col_top)
    col_totals = jnp.sum(shifted, axis=0, keepdims=True)
    chosen = (doc_ids[:, None] == goal_ids[None, :]).astype(jnp.float32)
    losses = col_top[0] + jnp.log(col_totals[0]) - jnp.sum(chosen * logits, axis=0)
    d_logits = shifted / col_totals - chosen
    d_pooled = (score_scale * d_logits / divisor)[:, :, None] * valid_mask.reshape(
        1, query_count, slot_count
    )
    return (losses, d_pooled.reshape(wide_count, token_count))


def local(
    doc_tokens,
    query_tokens,
    query_lengths,
    retrieved,
    targets,
    q_weight,
    k_weight,
    v_weight,
    o_weight,
    gate_weight,
    up_weight,
    down_weight,
    proj_weight,
    attn_gain,
    ffn_gain,
    final_gain,
    rel_bias,
):
    micro_count = doc_tokens.shape[0]
    doc_len = doc_tokens.shape[2]
    slot_count = query_tokens.shape[2]
    picks_width = retrieved.shape[3]
    bias_table = rel_bias.astype(jnp.float32)
    onehot_doc = bucket_onehot(doc_len, rel_bias.shape[0])
    onehot_query = bucket_onehot(slot_count, rel_bias.shape[0])
    bias_doc = jnp.einsum("ijb,bh->hij", onehot_doc, bias_table, precision=top_precision)
    bias_query = jnp.einsum("ijb,bh->hij", onehot_query, bias_table, precision=top_precision)
    doc_valid = jnp.ones((1, doc_len), dtype=bool)
    slot_ids = jnp.arange(slot_count, dtype=jnp.int32)
    positions = lax.axis_index("wide") * doc_len + jnp.arange(doc_len, dtype=jnp.int32)
    wide_count = lax.axis_size("wide")
    picks_group = lax.all_gather(retrieved, "wide", axis=1, tiled=True)
    loss_list = []
    doc_grad_list = []
    query_grad_list = []
    table_total = jnp.zeros(rel_bias.shape, jnp.float32)
    for micro_step in range(micro_count):
        full_weights = (
            lax.all_gather(q_weight, ("dp", "wide"), axis=0, tiled=True),
            lax.all_gather(k_weight, ("dp", "wide"), axis=0, tiled=True),
            lax.all_gather(v_weight, ("dp", "wide"), axis=0, tiled=True),
            lax.all_gather(o_weight, ("dp", "wide"), axis=0, tiled=True),
            lax.all_gather(gate_weight, ("dp", "wide"), axis=0, tiled=True),
            lax.all_gather(up_weight, ("dp", "wide"), axis=0, tiled=True),
            lax.all_gather(down_weight, ("dp", "wide"), axis=0, tiled=True),
            lax.all_gather(proj_weight, ("dp", "wide"), axis=0, tiled=True),
            lax.all_gather(attn_gain, ("dp", "wide"), axis=0, tiled=True),
            lax.all_gather(ffn_gain, ("dp", "wide"), axis=0, tiled=True),
            lax.all_gather(final_gain, ("dp", "wide"), axis=0, tiled=True),
        )
        query_valid = slot_ids[None, :] < query_lengths[micro_step][:, None]
        doc_emb, doc_state = encode_forward(
            doc_tokens[micro_step], doc_valid, bias_doc, full_weights
        )
        query_emb, query_state = encode_forward(
            query_tokens[micro_step], query_valid, bias_query, full_weights
        )
        query_all = lax.all_gather(query_emb, "wide", axis=0, tiled=True)
        picks_all = picks_group[micro_step].reshape(-1, picks_width)
        pooled = score_forward(query_all, picks_all, doc_emb, positions)
        pooled_query = lax.all_to_all(
            pooled.reshape(wide_count, -1), "wide", split_axis=0, concat_axis=0, tiled=True
        )
        own_picks = retrieved[micro_step].reshape(-1, picks_width)
        losses, d_pooled = query_loss(
            pooled_query, own_picks, query_lengths[micro_step], targets[micro_step], doc_len
        )
        d_pooled_doc = lax.all_to_all(d_pooled, "wide", split_axis=0, concat_axis=0, tiled=True)
        doc_emb_grad, query_all_grad = score_backward(
            query_all, picks_all, doc_emb, positions, d_pooled_doc.reshape(-1)
        )
        query_emb_grad = sent_and_summed(query_all_grad.astype(jnp.bfloat16), "wide", 0)
        doc_in_grad, doc_weight_grads, doc_table = encode_backward(
            doc_emb_grad, doc_state, doc_valid, bias_doc, onehot_doc, full_weights
        )
        query_in_grad, query_weight_grads, query_table = encode_backward(
            query_emb_grad, query_state, query_valid, bias_query, onehot_query, full_weights
        )
        step_grads = jax.tree.map(jnp.add, doc_weight_grads, query_weight_grads)
        table_total = table_total + doc_table + query_table
        loss_list.append(losses)
        doc_grad_list.append(doc_in_grad.reshape(doc_tokens.shape[1:]))
        query_grad_list.append(query_in_grad.reshape(query_tokens.shape[1:]))
        step_shards = (
            lax.psum_scatter(step_grads[0], ("dp", "wide"), scatter_dimension=0, tiled=True),
            lax.psum_scatter(step_grads[1], ("dp", "wide"), scatter_dimension=0, tiled=True),
            lax.psum_scatter(step_grads[2], ("dp", "wide"), scatter_dimension=0, tiled=True),
            lax.psum_scatter(step_grads[3], ("dp", "wide"), scatter_dimension=0, tiled=True),
            lax.psum_scatter(step_grads[4], ("dp", "wide"), scatter_dimension=0, tiled=True),
            lax.psum_scatter(step_grads[5], ("dp", "wide"), scatter_dimension=0, tiled=True),
            lax.psum_scatter(step_grads[6], ("dp", "wide"), scatter_dimension=0, tiled=True),
            lax.psum_scatter(step_grads[7], ("dp", "wide"), scatter_dimension=0, tiled=True),
            lax.psum_scatter(step_grads[8], ("dp", "wide"), scatter_dimension=0, tiled=True),
            lax.psum_scatter(step_grads[9], ("dp", "wide"), scatter_dimension=0, tiled=True),
            lax.psum_scatter(step_grads[10], ("dp", "wide"), scatter_dimension=0, tiled=True),
        )
        shard_total = (
            step_shards if micro_step == 0 else jax.tree.map(jnp.add, shard_total, step_shards)
        )
    table_grad = lax.psum(table_total, ("dp", "wide"))
    losses_out = jnp.stack(loss_list)
    doc_grad_out = jnp.stack(doc_grad_list)
    query_grad_out = jnp.stack(query_grad_list)
    return (
        losses_out,
        doc_grad_out,
        query_grad_out,
        shard_total[0],
        shard_total[1],
        shard_total[2],
        shard_total[3],
        shard_total[4],
        shard_total[5],
        shard_total[6],
        shard_total[7],
        shard_total[8],
        shard_total[9],
        shard_total[10],
        table_grad,
    )


def solution(mesh):
    placed = (
        P(None, ("dp", "wide"), None, None),
        P(None, ("dp", "wide"), None, None),
        P(None, ("dp", "wide")),
        P(None, ("dp", "wide"), None, None),
        P(None, ("dp", "wide")),
        P(("dp", "wide"), None),
        P(("dp", "wide"), None),
        P(("dp", "wide"), None),
        P(("dp", "wide"), None),
        P(("dp", "wide"), None),
        P(("dp", "wide"), None),
        P(("dp", "wide"), None),
        P(("dp", "wide"), None),
        P(("dp", "wide")),
        P(("dp", "wide")),
        P(("dp", "wide")),
        P(),
    )
    return jax.shard_map(
        local,
        mesh=mesh,
        in_specs=placed,
        out_specs=(
            P(None, ("dp", "wide")),
            P(None, ("dp", "wide"), None, None),
            P(None, ("dp", "wide"), None, None),
            P(("dp", "wide"), None),
            P(("dp", "wide"), None),
            P(("dp", "wide"), None),
            P(("dp", "wide"), None),
            P(("dp", "wide"), None),
            P(("dp", "wide"), None),
            P(("dp", "wide"), None),
            P(("dp", "wide"), None),
            P(("dp", "wide")),
            P(("dp", "wide")),
            P(("dp", "wide")),
            P(),
        ),
        check_vma=False,
    )
```

profile of v0, /device:TPU:1, one launch (start us, length us, event | category | flops | bytes accessed | tf_op | source)
XLA Modules:
  0.0 1565.0 jit_solution(3283499926414398930)
XLA Ops:
  12.7 16.7 %all_gather.53 = s32[2,16,32,32]{3,2,1,0:T(8,128)S(1)} all-gather(s32[2,2,32,32]{3,2,1,0:T(8,128)} %param.20), channel_id=1, replica_groups=mesh['dp'=4,'wide'=8] {'wide'}, dimensions={1}, use_global_device_ids=true | all-gather | bytes 147456 | tf_op jit(solution)/shard_map/all_gather | solution.py:375
  34.1 20.1 %convert_reduce_fusion.2 = (f32[512]{0:T(512)}, f32[512,512]{1,0:T(8,128)}, f32[512,512]{1,0:T(8,128)}, f32[512]{0:T(512)}) fusion(s32[512]{0:T(512)S(1)} %iota_add_fusion, s32[512,32]{1,0:T(8,128)S(1)} %bitcast.517, s32[512,32]{1,0:T(8,128)S(1)} %bitcast.516), kind=kLoop, calls=%fused_computation.2 | loop fusion | flops 66583552 | bytes 2234368 | tf_op jit(solution)/shard_map/while/body/eval_jaxpr/reduce_sum | solution.py:261
  56.9 42.4 %all_gather.64 = bf16[768,128]{1,0:T(8,128)(2,1)S(1)} all-gather(bf16[24,128]{1,0:T(8,128)(2,1)S(1)} %copy-done.230), channel_id=1, replica_groups=mesh['dp'=4,'wide'=8] {'dp','wide'}, dimensions={0}, use_global_device_ids=true | all-gather | bytes 202752 | tf_op jit(solution)/shard_map/all_gather | solution.py:389
  100.7 36.1 %all-reduce.8 = (bf16[768]{0:T(1024)(128)(2,1)S(1)}, bf16[768]{0:T(1024)(128)(2,1)S(1)}, bf16[768]{0:T(1024)(128)(2,1)S(1)}) all-reduce(bf16[768]{0:T(1024)(128)(2,1)S(1)} %dynamic-update-slice, bf16[768]{0:T(1024)(128)(2,1)S(1)} %dynamic-update-slice.1, ...), channel_id=1, replica_groups=mesh['dp'=4,'wide'=8] {'dp','wide'}, use_global_device_ids=true, to_apply=%add | all-reduce | flops 2304 | bytes 9216
  148.4 18.0 %copy.187 = f32[512,512,12]{0,1,2:T(8,128)} copy(f32[512,512,12]{1,2,0:T(8,128)} %fusion.2) | data formatting | bytes 25165824 | tf_op jit(solution)/shard_map/ijb,bh->hij/dot_general | solution.py:369
  227.5 8.8 all-gather.14.cloned.1.call-done
  276.9 20.2 %all-gather.16.cloned.1.call-done = bf16[768,2048]{1,0:T(8,128)(2,1)} async-done(((bf16[24,2048]{1,0:T(8,128)(2,1)}), bf16[768,2048]{1,0:T(8,128)(2,1)}) %all-gather.16.cloned.1.call-update) | async-done | bytes 3145744 | tf_op jit(solution)/shard_map/all_gather | solution.py:386
  299.7 58.3 %all-gather.18.cloned.1.call-done = bf16[768,2048]{1,0:T(8,128)(2,1)} async-done(((bf16[24,2048]{1,0:T(8,128)(2,1)}), bf16[768,2048]{1,0:T(8,128)(2,1)}) %all-gather.18.cloned.1.call-update) | async-done | bytes 3145744 | tf_op jit(solution)/shard_map/all_gather | solution.py:387
  361.6 57.4 %all-gather.20.cloned.1.call-done = bf16[2048,768]{1,0:T(8,128)(2,1)} async-done(((bf16[64,768]{1,0:T(8,128)(2,1)}), bf16[2048,768]{1,0:T(8,128)(2,1)}) %all-gather.20.cloned.1.call-update) | async-done | bytes 3145744 | tf_op jit(solution)/shard_map/all_gather | solution.py:388
  422.5 14.2 all_gather.65
  523.4 11.3 multiply_reduce_fusion.1
  565.6 14.4 all_gather.66
  642.8 10.7 multiply_reduce_fusion
  802.9 19.2 %copy.230 = f32[12,512,512]{2,0,1:T(8,128)} copy(f32[12,512,512]{1,2,0:T(8,128)} %copy-done.4) | data formatting | bytes 25165824 | tf_op jit(solution)/shard_map/mul | solution.py:216
  826.2 20.7 %fusion.111 = f32[32,12]{0,1:T(8,128)} fusion(f32[12,512,512]{2,0,1:T(8,128)} %copy.230, s32[512,512]{1,0:T(8,128)S(1)} %copy-done.20), kind=kOutput, calls=%fused_computation.212 | convolution fusion | flops 1216348160 | bytes 13633024 | tf_op jit(solution)/shard_map/hij,ijb->bh/dot_general | solution.py:217
  853.1 18.6 %copy.232 = f32[12,512,512]{2,0,1:T(8,128)} copy(f32[12,512,512]{1,2,0:T(8,128)} %copy-done.5) | data formatting | bytes 25165824 | tf_op jit(solution)/shard_map/mul | solution.py:216
  882.5 17.5 %fusion.112 = f32[32,12]{0,1:T(8,128)S(1)} fusion(f32[12,512,512]{2,0,1:T(8,128)S(1)} %bitcast.481, s32[512,512]{1,0:T(8,128)S(1)} %copy-done.21), kind=kOutput, calls=%fused_computation.213 | convolution fusion | flops 1216348160 | bytes 13633024 | tf_op jit(solution)/shard_map/hij,ijb->bh/dot_general | solution.py:217
  906.8 39.7 %all-reduce.7 = (f32[768]{0:T(1024)S(1)}, f32[768]{0:T(1024)S(1)}, f32[768]{0:T(1024)S(1)}, f32[32,12]{0,1:T(8,128)}) all-reduce(f32[768]{0:T(1024)S(1)} %add_add_fusion.11, f32[768]{0:T(1024)S(1)} %add_add_fusion.10, f32[768]{0:T(1024)S(1)} %add_add_fusion.9, ...), channel_id=21, replica_groups=mesh['dp'=4,'wide'=8] {'dp','wide'}, use_global_device_ids=true, to_apply=%region_74.75.clone | all-reduce | flops 2688 | bytes 21504
  949.2 39.6 %reduce-scatter.13.cloned.1.call-done = f32[24,768]{1,0:T(8,128)} async-done(((f32[768,768]{1,0:T(8,128)}), f32[24,768]{1,0:T(8,128)}) %reduce-scatter.13.cloned.1.call-update) | async-done | bytes 73744 | tf_op jit(solution)/shard_map/reduce_scatter | solution.py:429
  988.8 104.8 %reduce-scatter.15.cloned.1.call-done = f32[24,768]{1,0:T(8,128)} async-done(((f32[768,768]{1,0:T(8,128)}), f32[24,768]{1,0:T(8,128)}) %reduce-scatter.15.cloned.1.call-update) | async-done | bytes 73744 | tf_op jit(solution)/shard_map/reduce_scatter | solution.py:430
  1093.6 103.8 %reduce-scatter.17.cloned.1.call-done = f32[24,768]{1,0:T(8,128)} async-done(((f32[768,768]{1,0:T(8,128)}), f32[24,768]{1,0:T(8,128)}) %reduce-scatter.17.cloned.1.call-update) | async-done | bytes 73744 | tf_op jit(solution)/shard_map/reduce_scatter | solution.py:431
  1197.4 120.5 %reduce-scatter.19.cloned.1.call-done = f32[24,2048]{1,0:T(8,128)} async-done(((f32[768,2048]{1,0:T(8,128)}), f32[24,2048]{1,0:T(8,128)}) %reduce-scatter.19.cloned.1.call-update) | async-done | bytes 196624 | tf_op jit(solution)/shard_map/reduce_scatter | solution.py:432
  1317.8 119.8 %reduce-scatter.21.cloned.1.call-done = f32[24,2048]{1,0:T(8,128)} async-done(((f32[768,2048]{1,0:T(8,128)}), f32[24,2048]{1,0:T(8,128)}) %reduce-scatter.21.cloned.1.call-update) | async-done | bytes 196624 | tf_op jit(solution)/shard_map/reduce_scatter | solution.py:433
  1437.6 120.7 %reduce-scatter.23.cloned.1.call-done = f32[64,768]{1,0:T(8,128)} async-done(((f32[2048,768]{1,0:T(8,128)}), f32[64,768]{1,0:T(8,128)}) %reduce-scatter.23.cloned.1.call-update) | async-done | bytes 196624 | tf_op jit(solution)/shard_map/reduce_scatter | solution.py:434
  (875 shorter events, 494.5 us)
Async XLA Ops:
  7.2 92.1 %copy-start = (bf16[32,12]{0,1:T(8,128)(2,1)S(1)}, bf16[32,12]{0,1:T(8,128)(2,1)}, u32[]{:S(2)}) copy-start(bf16[32,12]{0,1:T(8,128)(2,1)} %param.33) | copy-start | bytes 2308
  7.2 163.7 %all-gather.12.cloned.1.call-start = ((), (), s32[]{:S(2)}) async-start(), calls=%async_computation.16 | async-start | bytes 1216512 | tf_op jit(solution)/shard_map/all_gather | solution.py:383
  7.9 164.8 %all-gather.10.cloned.1.call-start = ((), (), s32[]{:S(2)}) async-start(), calls=%async_computation.15 | async-start | bytes 1216512 | tf_op jit(solution)/shard_map/all_gather | solution.py:382
  8.7 171.5 %all-gather.8.cloned.1.call-start = ((), (), s32[]{:S(2)}) async-start(), calls=%async_computation.14 | async-start | bytes 1216512 | tf_op jit(solution)/shard_map/all_gather | solution.py:384
  9.4 226.8 %all-gather.14.cloned.1.call-start = ((), (), s32[]{:S(2)}) async-start(), calls=%async_computation.17 | async-start | bytes 1216512 | tf_op jit(solution)/shard_map/all_gather | solution.py:385
  10.0 287.1 %all-gather.16.cloned.1.call-start = ((), (), s32[]{:S(2)}) async-start(), calls=%async_computation.18 | async-start | bytes 3244032 | tf_op jit(solution)/shard_map/all_gather | solution.py:386
  10.6 347.4 %all-gather.18.cloned.1.call-start = ((), (), s32[]{:S(2)}) async-start(), calls=%async_computation.19 | async-start | bytes 3244032 | tf_op jit(solution)/shard_map/all_gather | solution.py:387
  11.2 407.8 %all-gather.20.cloned.1.call-start = ((), (), s32[]{:S(2)}) async-start(), calls=%async_computation.20 | async-start | bytes 3244032 | tf_op jit(solution)/shard_map/all_gather | solution.py:388
  33.1 106.9 %copy-start.19 = (s32[512,512]{1,0:T(8,128)}, s32[512,512]{1,0:T(8,128)S(1)}, u32[]{:S(2)}) copy-start(s32[512,512]{1,0:T(8,128)S(1)} %fusion.116) | copy-start | bytes 3145732
  451.9 8.7 all-to-all-start
  470.5 9.5 all-to-all-start.2
  490.9 60.5 %all-to-all-start.4 = ((bf16[8,64,128]{2,1,0:T(8,128)(2,1)}), bf16[8,64,128]{2,1,0:T(8,128)(2,1)}, u32[]{:S(2)}, u32[]{:S(2)}) async-start(bf16[8,64,128]{2,1,0:T(8,128)(2,1)} %bitcast.526), calls=%async_computation.4 | async-start | bytes 262144 | tf_op jit(solution)/shard_map/all_to_all | solution.py:21
  583.9 15.8 %all-to-all-start.1 = ((f32[8,1,64]{2,1,0:T(1,128)}), f32[8,1,64]{2,1,0:T(1,128)}, u32[]{:S(2)}, u32[]{:S(2)}) async-start(f32[8,1,64]{2,1,0:T(1,128)} %log.88), calls=%async_computation.1 | async-start | bytes 8192 | tf_op jit(solution)/shard_map/all_to_all | solution.py:404
  607.1 10.0 all-to-all-start.3
  667.6 10.0 all-to-all-start.5
  671.7 277.5 %reduce-scatter.25.cloned.1.call-start = ((), (), s32[]{:S(2)}) async-start(), calls=%async_computation.28 | async-start | bytes 405504
  688.0 261.2 %reduce-scatter.11.cloned.1.call-start = ((), (), s32[]{:S(2)}) async-start(), calls=%async_computation.21 | async-start | bytes 2433024 | tf_op jit(solution)/shard_map/reduce_scatter | solution.py:428
  695.4 293.4 %reduce-scatter.13.cloned.1.call-start = ((), (), s32[]{:S(2)}) async-start(), calls=%async_computation.22 | async-start | bytes 2433024 | tf_op jit(solution)/shard_map/reduce_scatter | solution.py:429
  725.1 368.6 %reduce-scatter.15.cloned.1.call-start = ((), (), s32[]{:S(2)}) async-start(), calls=%async_computation.23 | async-start | bytes 2433024 | tf_op jit(solution)/shard_map/reduce_scatter | solution.py:430
  754.9 442.4 %reduce-scatter.17.cloned.1.call-start = ((), (), s32[]{:S(2)}) async-start(), calls=%async_computation.24 | async-start | bytes 2433024 | tf_op jit(solution)/shard_map/reduce_scatter | solution.py:431
  762.8 555.0 %reduce-scatter.19.cloned.1.call-start = ((), (), s32[]{:S(2)}) async-start(), calls=%async_computation.25 | async-start | bytes 6488064 | tf_op jit(solution)/shard_map/reduce_scatter | solution.py:432
  774.8 662.8 %reduce-scatter.21.cloned.1.call-start = ((), (), s32[]{:S(2)}) async-start(), calls=%async_computation.26 | async-start | bytes 6488064 | tf_op jit(solution)/shard_map/reduce_scatter | solution.py:433
  785.6 772.7 %reduce-scatter.23.cloned.1.call-start = ((), (), s32[]{:S(2)}) async-start(), calls=%async_computation.27 | async-start | bytes 6488064 | tf_op jit(solution)/shard_map/reduce_scatter | solution.py:434
  903.3 655.0 %copy-start.1 = (bf16[32,12]{0,1:T(8,128)(2,1)S(1)}, bf16[32,12]{0,1:T(8,128)(2,1)}, u32[]{:S(2)}) copy-start(bf16[32,12]{0,1:T(8,128)(2,1)} %param.33) | copy-start | bytes 2308
  (263 other events, 1915.0 us)
Sparse Core Ops, SparseCore 0:
  11.1 56.8 all-gather.11
  70.9 53.0 all-gather.9
  127.1 53.0 all-gather.7
  183.1 53.1 all-gather.13
  239.1 57.9 all-gather.15
  300.0 57.9 all-gather.17
  361.0 57.9 all-gather.19
  688.1 91.3 reduce-scatter.24
  786.2 98.4 reduce-scatter.10
  890.4 98.3 reduce-scatter.12
  995.5 98.0 reduce-scatter.14
  1099.3 97.9 reduce-scatter.16
  1204.5 113.2 reduce-scatter.18
  1323.9 113.6 reduce-scatter.20
  1444.6 113.6 reduce-scatter.22
where the time goes:
time: 1580 us; the launch traced here: 1570 us
  waiting for transfers between devices  774 us (49%)
  matrix products  337 us (21%)
  blocking collectives  163 us (10%)
  local copies, waits for them, and re-layouts  153 us (10%)
  other arithmetic  90.9 us (6%)
  starting transfers between devices  28.7 us (2%)
  between operations  17.2 us (1%)
    reduce_scatter x1, waiting for transfers between devices, local(): lax.psum_scatter(step_grads[6], ('dp', 'wide'), scatter_dimension=0, tile...  121 us
    reduce_scatter x1, waiting for transfers between devices, local(): lax.psum_scatter(step_grads[4], ('dp', 'wide'), scatter_dimension=0, tile...  120 us
    reduce_scatter x1, waiting for transfers between devices, local(): lax.psum_scatter(step_grads[5], ('dp', 'wide'), scatter_dimension=0, tile...  120 us
    reduce_scatter x1, waiting for transfers between devices, local(): lax.psum_scatter(step_grads[2], ('dp', 'wide'), scatter_dimension=0, tile...  105 us
    reduce_scatter x1, waiting for transfers between devices, local(): lax.psum_scatter(step_grads[3], ('dp', 'wide'), scatter_dimension=0, tile...  104 us
    unnamed x2, blocking collectives  75.7 us
    dot_general x34, matrix products, contract_rows(): lax.dot_general(left_mat, right_mat, (((0,), (0,)), ((), ())), preferred_...  75.1 us
    dot_general x34, matrix products, contract_cols(): lax.dot_general(left_mat, right_mat, (((1,), (1,)), ((), ())), preferred_...  69.4 us
  transfers between devices with their start and end apart: 21, of which 15 were waited for; matrix products, arithmetic and copies ran while one was open for 27% of the time, Pallas kernels for 0%

commit v1 on v0

--- a/solution.py
+++ b/solution.py
@@ -1,6 +1,10 @@
+import functools
+
 import jax
 import jax.numpy as jnp
 from jax import lax
+from jax.experimental import pallas as pl
+from jax.experimental.pallas import tpu as pltpu
 from jax.sharding import PartitionSpec as P
 
 eps_norm = 1e-06
@@ -8,6 +12,465 @@
 mask_fill = -1000000000.0
 top_precision = lax.Precision.HIGHEST
 block_rows = 512
+
+
+MESH = pl.DeviceIdType.MESH
+
+def gray(p):
+    return p + (p // 2) * (1 - 2 * (p % 2))
+
+class Place:
+    def __init__(self, zc):
+        self.zc = zc
+        d = lax.axis_index("dp"); w = lax.axis_index("wide")
+        self.d, self.w = d, w
+        self.z, self.c = w // 2, w % 2
+        p = gray(d)
+        self.right = gray((p + 1) % 4); self.left = gray((p + 3) % 4); self.opp = gray((p + 2) % 4)
+    def dev(self, d=None, z=None, c=None):
+        d = self.d if d is None else d
+        z = self.z if z is None else z
+        c = self.c if c is None else c
+        return (d, z * 2 + c)
+
+def enter(pos):
+    barrier = pltpu.get_barrier_semaphore()
+    for dev in (pos.dev(d=pos.right), pos.dev(d=pos.left), pos.dev(c=1 - pos.c)):
+        pl.semaphore_signal(barrier, inc=1, device_id=dev, device_id_type=MESH)
+    @pl.when(pos.z > 0)
+    def _():
+        pl.semaphore_signal(barrier, inc=1, device_id=pos.dev(z=pos.z - 1), device_id_type=MESH)
+    @pl.when(pos.z < pos.zc - 1)
+    def _():
+        pl.semaphore_signal(barrier, inc=1, device_id=pos.dev(z=pos.z + 1), device_id_type=MESH)
+    zc = pos.zc
+    peers = 3 + (pos.z + zc - 1) // zc + (2 * zc - 2 - pos.z) // zc
+    pl.semaphore_wait(barrier, peers)
+
+def gather_kernel(zc, count, *refs):
+    pos = Place(zc)
+    shard = refs[:count]
+    out = refs[count:2 * count]
+    rest = refs[2 * count:]
+    comp = rest[:count]; mine = rest[count:2 * count]
+    (s_col, s_ring, s_fwd, s_mate, s_pair, s_own, r_col, r_left, r_right, r_opp, r_mate, r_pair) = rest[2 * count:]
+    z, c, d = pos.z, pos.c, pos.d
+    enter(pos)
+    rows = [o.shape[0] // (4 * zc) for o in out]
+    half = [o.shape[1] // 2 for o in out]
+
+    def part(a, ref, blk, core):
+        return ref.at[pl.ds(pl.multiple_of(blk * rows[a], 16), rows[a]), pl.ds(pl.multiple_of(core * half[a], 128), half[a])]
+    def own(a, core):
+        return comp[a].at[:, pl.ds(pl.multiple_of(core * half[a], 128), half[a])]
+    def rdma(a, src, blk, dev, ss, rs):
+        return pltpu.make_async_remote_copy(src_ref=src, dst_ref=part(a, out[a], blk, c), send_sem=ss, recv_sem=rs, device_id=dev, device_id_type=MESH)
+    def blk(dd, zz):
+        return dd * zc + zz
+    mate_dev = pos.dev(c=1 - c)
+    def pair(a):
+        return pltpu.make_async_remote_copy(src_ref=shard[a], dst_ref=mine[a], send_sem=s_pair.at[a], recv_sem=r_pair.at[a], device_id=mate_dev, device_id_type=MESH)
+    def keep(a):
+        return pltpu.make_async_copy(comp[a], out[a].at[pl.ds(pl.multiple_of(blk(d, z) * rows[a], 16), rows[a]), :], s_own.at[a])
+    def up(a, src, zz):
+        return rdma(a, src, blk(d, zz), pos.dev(z=lax.rem(z + 1, zc)), s_col.at[a, 0, zz], r_col.at[a, zz])
+    def down(a, src, zz):
+        return rdma(a, src, blk(d, zz), pos.dev(z=lax.rem(z + zc - 1, zc)), s_col.at[a, 1, zz], r_col.at[a, zz])
+    def right(a, src, zz):
+        return rdma(a, src, blk(d, zz), pos.dev(d=pos.right), s_ring.at[a, 0, zz], r_left.at[a, zz])
+    def left(a, src, zz):
+        return rdma(a, src, blk(d, zz), pos.dev(d=pos.left), s_ring.at[a, 1, zz], r_right.at[a, zz])
+    def fwd_right(a, zz):
+        b = blk(pos.left, zz)
+        return rdma(a, part(a, out[a], b, c), b, pos.dev(d=pos.right), s_fwd.at[a, zz], r_opp.at[a, zz])
+    def fwd_left(a, zz):
+        b = blk(pos.right, zz)
+        return rdma(a, part(a, out[a], b, c), b, pos.dev(d=pos.left), s_fwd.at[a, zz], r_opp.at[a, zz])
+    def mate(a, b):
+        return rdma(a, part(a, out[a], b, c), b, mate_dev, s_mate.at[a, b], r_mate.at[a, b])
+    def got(a, b, sem):
+        return rdma(a, part(a, out[a], b, c), b, mate_dev, s_mate.at[a, b], sem).wait_recv()
+    def mate_got(a, b):
+        piece = part(a, out[a], b, 1 - c)
+        pltpu.make_async_remote_copy(src_ref=piece, dst_ref=piece, send_sem=s_mate.at[a, b], recv_sem=r_mate.at[a, b], device_id=mate_dev, device_id_type=MESH).wait_recv()
+
+    for a in range(count):
+        pair(a).start()
+    for a in range(count):
+        pair(a).wait_recv()
+        r2 = rows[a] // 2
+        step = 256 if half[a] * 2 % 256 == 0 else 128
+        @pl.loop(0, half[a] * 2 // step)
+        def _(t):
+            cols = pl.ds(pl.multiple_of(t * step, 128), step)
+            mn = shard[a][:, cols].astype(jnp.float32)[:r2]
+            ot = mine[a][:, cols].astype(jnp.float32)[:r2]
+            first = jnp.where(c == 0, mn, ot)
+            second = jnp.where(c == 0, ot, mn)
+            comp[a][:, cols] = jnp.concatenate([first, second], axis=0).astype(jnp.bfloat16)
+        right(a, own(a, c), z).start()
+        left(a, own(a, c), z).start()
+        pl.when(z < zc - 1)(lambda: up(a, own(a, c), z).start())
+        pl.when(z > 0)(lambda: down(a, own(a, c), z).start())
+        keep(a).start()
+
+    def column(a, j):
+        @pl.when(z - j >= 0)
+        def _():
+            zz = z - j
+            got(a, blk(d, zz), r_col.at[a, zz])
+            src = part(a, out[a], blk(d, zz), c)
+            pl.when(z < zc - 1)(lambda: up(a, src, zz).start())
+            right(a, src, zz).start(); left(a, src, zz).start()
+            mate(a, blk(d, zz)).start()
+        @pl.when(z + j < zc)
+        def _():
+            zz = z + j
+            got(a, blk(d, zz), r_col.at[a, zz])
+            src = part(a, out[a], blk(d, zz), c)
+            pl.when(z > 0)(lambda: down(a, src, zz).start())
+            right(a, src, zz).start(); left(a, src, zz).start()
+            mate(a, blk(d, zz)).start()
+    def ring_one(a, zz):
+        got(a, blk(pos.left, zz), r_left.at[a, zz])
+        pl.when(zz % 2 == 0)(lambda: fwd_right(a, zz).start())
+        mate(a, blk(pos.left, zz)).start()
+        got(a, blk(pos.right, zz), r_right.at[a, zz])
+        pl.when(zz % 2 == 1)(lambda: fwd_left(a, zz).start())
+        mate(a, blk(pos.right, zz)).start()
+    def opp_one(a, zz):
+        got(a, blk(pos.opp, zz), r_opp.at[a, zz])
+        mate(a, blk(pos.opp, zz)).start()
+    def spread(fn, a, j):
+        if j == 0:
+            fn(a, z); return
+        pl.when(z - j >= 0)(lambda: fn(a, z - j))
+        pl.when(z + j < zc)(lambda: fn(a, z + j))
+    for a in range(count):
+        for t in range(zc + 2):
+            if 1 <= t < zc:
+                column(a, t)
+            if 1 <= t <= zc:
+                spread(ring_one, a, t - 1)
+            if 2 <= t:
+                spread(opp_one, a, t - 2)
+    for a in range(count):
+        pair(a).wait_send(); keep(a).wait()
+        @pl.loop(0, zc)
+        def _(zz):
+            src = part(a, out[a], blk(d, zz), c)
+            right(a, src, zz).wait_send(); left(a, src, zz).wait_send()
+            pl.when((z < zc - 1) & (zz <= z))(lambda: up(a, src, zz).wait_send())
+            pl.when((z > 0) & (zz >= z))(lambda: down(a, src, zz).wait_send())
+            fwd_right(a, zz).wait_send()
+        @pl.loop(0, 4 * zc)
+        def _(b):
+            @pl.when(b != blk(d, z))
+            def _():
+                mate(a, b).wait_send()
+                mate_got(a, b)
+
+def gather(shards, zc, n_dev):
+    count = len(shards)
+    outs, comps, mines = [], [], []
+    for s, rows in shards:
+        outs.append(jax.ShapeDtypeStruct((rows * n_dev, s.shape[1]), s.dtype))
+        comps.append(pltpu.VMEM((rows * 2, s.shape[1]), s.dtype))
+        mines.append(pltpu.VMEM(s.shape, s.dtype))
+    dma = pltpu.SemaphoreType.DMA
+    sems = [dma((count, 2, zc)), dma((count, 2, zc)), dma((count, zc)), dma((count, 4 * zc)), dma((count,)), dma((count,)),
+            dma((count, zc)), dma((count, zc)), dma((count, zc)), dma((count, zc)), dma((count, 4 * zc)), dma((count,))]
+    return pl.pallas_call(
+        functools.partial(gather_kernel, zc, count),
+        out_shape=outs,
+        in_specs=[pl.BlockSpec(memory_space=pltpu.VMEM)] * count,
+        out_specs=[pl.BlockSpec(memory_space=pl.ANY)] * count,
+        scratch_shapes=comps + mines + sems,
+        compiler_params=pltpu.CompilerParams(collective_id=0, has_side_effects=True, vmem_limit_bytes=32 << 20),
+        name="gather_weights",
+    )(*[s for s, _ in shards])
+
+
+F32 = jnp.float32; BF = jnp.bfloat16
+
+def reduce_kernel(zc, count, *refs):
+    pos = Place(zc)
+    z, c, d = pos.z, pos.c, pos.d
+    g = refs[:count]; table = refs[count]
+    out = refs[count + 1:2 * count + 1]; table_out = refs[2 * count + 1]
+    rest = refs[2 * count + 2:]
+    loc = rest[:count]; rxp = rest[count:2 * count]; rxf = rest[2 * count:3 * count]
+    rxl = rest[3 * count:4 * count]; rxr = rest[4 * count:5 * count]
+    rxu = rest[5 * count:6 * count]; rxd = rest[6 * count:7 * count]
+    fin = rest[7 * count:8 * count]; rxm = rest[8 * count:9 * count]
+    (tabs, s_tab, r_tab, s_pair, r_pair, s_loc, s_ring, r_fwd, r_left, r_right, s_z, r_up, r_dn, s_fin, r_fin) = rest[9 * count:]
+    rows = [x.shape[0] // (4 * zc) for x in g]
+    half = [x.shape[1] // 2 for x in g]
+    n_dev = 8 * zc
+    me = d * (2 * zc) + pos.w
+    barrier = pltpu.get_barrier_semaphore()
+    @pl.loop(1, n_dev)
+    def _(k):
+        o = lax.rem(me + k, n_dev)
+        pl.semaphore_signal(barrier, inc=1, device_id=(o // (2 * zc), lax.rem(o, 2 * zc)), device_id_type=MESH)
+    pl.semaphore_wait(barrier, n_dev - 1)
+    mate_dev = pos.dev(c=1 - c)
+    right_dev = pos.dev(d=pos.right); left_dev = pos.dev(d=pos.left)
+    def remote(src, dst, ss, rs, dev):
+        return pltpu.make_async_remote_copy(src_ref=src, dst_ref=dst, send_sem=ss, recv_sem=rs, device_id=dev, device_id_type=MESH)
+    def tab_copy(k):
+        o = lax.rem(me + k, n_dev)
+        return remote(table, tabs.at[me], s_tab.at[k], r_tab.at[me], (o // (2 * zc), lax.rem(o, 2 * zc)))
+    def tab_got(k):
+        o = lax.rem(me + k, n_dev)
+        return remote(table, tabs.at[o], s_tab.at[k], r_tab.at[o], (o // (2 * zc), lax.rem(o, 2 * zc)))
+    def strip(a, dd):
+        return pl.ds(pl.multiple_of(dd * zc * rows[a], 16), zc * rows[a])
+    def cols(a, core):
+        return pl.ds(pl.multiple_of(core * half[a], 128), half[a])
+    def pair(a, dd):
+        return remote(g[a].at[strip(a, dd), cols(a, 1 - c)], rxp[a].at[strip(a, dd), :], s_pair.at[a, dd], r_pair.at[a, dd], mate_dev)
+    def local(a, dd):
+        return pltpu.make_async_copy(g[a].at[strip(a, dd), cols(a, c)], loc[a].at[strip(a, dd), :], s_loc.at[a, dd])
+    def row(a, dd, zz):
+        return pl.ds(pl.multiple_of((dd * zc + zz) * rows[a], 16), rows[a])
+    def slot(a, zz):
+        return pl.ds(pl.multiple_of(zz * rows[a], 16), rows[a])
+    def add(a, dst, terms, out_ref=None):
+        step = 128 if half[a] % 256 else 256
+        @pl.loop(0, half[a] // step)
+        def _(t):
+            cc = pl.ds(pl.multiple_of(t * step, 128), step)
+            total = None
+            for ref, rr in terms:
+                v = ref[rr, cc].astype(F32)
+                total = v if total is None else total + v
+            dst[0][dst[1], cc] = total.astype(dst[0].dtype)
+    def pair_sum(a, dd, zz, extra=()):
+        r = row(a, dd, zz)
+        add(a, (loc[a], r), [(loc[a], r), (rxp[a], r)] + list(extra))
+    def first_right(a, zz):
+        return remote(loc[a].at[row(a, pos.opp, zz), :], rxf[a].at[slot(a, zz), :], s_ring.at[a, 0, zz], r_fwd.at[a, zz], right_dev)
+    def first_left(a, zz):
+        return remote(loc[a].at[row(a, pos.opp, zz), :], rxf[a].at[slot(a, zz), :], s_ring.at[a, 0, zz], r_fwd.at[a, zz], left_dev)
+    def to_right(a, zz):
+        return remote(loc[a].at[row(a, pos.right, zz), :], rxl[a].at[slot(a, zz), :], s_ring.at[a, 1, zz], r_left.at[a, zz], right_dev)
+    def to_left(a, zz):
+        return remote(loc[a].at[row(a, pos.left, zz), :], rxr[a].at[slot(a, zz), :], s_ring.at[a, 2, zz], r_right.at[a, zz], left_dev)
+    def up(a, zt):
+        return remote(loc[a].at[row(a, d, zt), :], rxu[a].at[slot(a, zt), :], s_z.at[a, zt], r_up.at[a, zt], pos.dev(z=lax.rem(z + 1, zc)))
+    def down(a, zt):
+        return remote(loc[a].at[row(a, d, zt), :], rxd[a].at[slot(a, zt), :], s_z.at[a, zt], r_dn.at[a, zt], pos.dev(z=lax.rem(z + zc - 1, zc)))
+    def mate_rows(a):
+        r2 = rows[a] // 2
+        return pl.ds(pl.multiple_of((1 - c) * r2, 8), r2)
+    def my_rows(a):
+        r2 = rows[a] // 2
+        return pl.ds(pl.multiple_of(c * r2, 8), r2)
+    def final(a):
+        return remote(fin[a].at[mate_rows(a), :], rxm[a], s_fin.at[a], r_fin.at[a], mate_dev)
+
+    for a in range(count):
+        for dd in (pos.opp, pos.right, pos.left, d):
+            pair(a, dd).start(); local(a, dd).start()
+    @pl.loop(1, n_dev)
+    def _(k):
+        tab_copy(k).start()
+
+    def phase_p(a):
+        dd = pos.opp
+        pair(a, dd).wait_recv(); local(a, dd).wait()
+        for zz in range(zc):
+            pair_sum(a, dd, zz)
+            (first_right if zz % 2 == 0 else first_left)(a, zz).start()
+        dd = pos.right
+        pair(a, dd).wait_recv(); local(a, dd).wait()
+        dd = pos.left
+        pair(a, dd).wait_recv(); local(a, dd).wait()
+        for zz in range(zc):
+            if zz % 2:
+                pair_sum(a, pos.right, zz); to_right(a, zz).start()
+            else:
+                pair_sum(a, pos.left, zz); to_left(a, zz).start()
+    def phase_q(a):
+        for zz in range(zc):
+            if zz % 2 == 0:
+                first_right(a, zz).wait_recv()
+                pair_sum(a, pos.right, zz, [(rxf[a], slot(a, zz))]); to_right(a, zz).start()
+            else:
+                first_left(a, zz).wait_recv()
+                pair_sum(a, pos.left, zz, [(rxf[a], slot(a, zz))]); to_left(a, zz).start()
+        pair(a, d).wait_recv(); local(a, d).wait()
+    def phase_r(a):
+        def column(zz, dst, extra=()):
+            r = row(a, d, zz)
+            add(a, dst, [(loc[a], r), (rxp[a], r), (rxl[a], slot(a, zz)), (rxr[a], slot(a, zz))] + list(extra))
+        def arrived(zz):
+            to_right(a, zz).wait_recv(); to_left(a, zz).wait_recv()
+        for zt in range(zc):
+            arrived(zt)
+        for i in range(zc - 1):
+            zt = zc - 1 - i
+            @pl.when(z < zt)
+            def _():
+                r = row(a, d, zt)
+                @pl.when(z > 0)
+                def _():
+                    up(a, zt).wait_recv()
+                    column(zt, (loc[a], r), [(rxu[a], slot(a, zt))])
+                @pl.when(z == 0)
+                def _():
+                    column(zt, (loc[a], r))
+                up(a, zt).start()
+            zs = i
+            @pl.when(z > zs)
+            def _():
+                r = row(a, d, zs)
+                @pl.when(z < zc - 1)
+                def _():
+                    down(a, zs).wait_recv()
+                    column(zs, (loc[a], r), [(rxd[a], slot(a, zs))])
+                @pl.when(z == zc - 1)
+                def _():
+                    column(zs, (loc[a], r))
+                down(a, zs).start()
+        full = (fin[a], slice(None))
+        zz = z
+        @pl.when(z > 0)
+        def _():
+            up(a, zz).wait_recv()
+        @pl.when(z < zc - 1)
+        def _():
+            down(a, zz).wait_recv()
+        @pl.when(z == 0)
+        def _():
+            column(zz, full, [(rxd[a], slot(a, zz))])
+        @pl.when(z == zc - 1)
+        def _():
+            column(zz, full, [(rxu[a], slot(a, zz))])
+        @pl.when((z > 0) & (z < zc - 1))
+        def _():
+            column(zz, full, [(rxu[a], slot(a, zz)), (rxd[a], slot(a, zz))])
+        final(a).start()
+    def phase_s(a):
+        out[a][:, cols(a, c)] = fin[a][my_rows(a), :]
+        final(a).wait_recv()
+        out[a][:, cols(a, 1 - c)] = rxm[a][...]
+    for t in range(count + 2):
+        if t < count: phase_p(t)
+        if 1 <= t <= count: phase_q(t - 1)
+        if 2 <= t: phase_r(t - 2)
+    for a in range(count):
+        phase_s(a)
+    tabs[me] = table[...]
+    @pl.loop(1, n_dev)
+    def _(k):
+        tab_got(k).wait_recv()
+        tab_copy(k).wait_send()
+    total = tabs[0]
+    for k in range(1, n_dev):
+        total = total + tabs[k]
+    table_out[...] = total
+    for a in range(count):
+        for dd in range(4):
+            pair(a, dd).wait_send()
+        for zz in range(zc):
+            (first_right if zz % 2 == 0 else first_left)(a, zz).wait_send()
+            to_right(a, zz).wait_send(); to_left(a, zz).wait_send()
+            @pl.when(zz != z)
+            def _():
+                up(a, zz).wait_send()
+        final(a).wait_send()
+
+def reduce_scatter(grads, table, zc):
+    count = len(grads)
+    n_dev = 8 * zc
+    V = pltpu.VMEM
+    outs = [jax.ShapeDtypeStruct((x.shape[0] // n_dev, x.shape[1]), F32) for x in grads] + [jax.ShapeDtypeStruct(table.shape, F32)]
+    rows = [x.shape[0] // (4 * zc) for x in grads]; half = [x.shape[1] // 2 for x in grads]
+    scratch = []
+    scratch += [V((x.shape[0], h), BF) for x, h in zip(grads, half)]
+    scratch += [V((x.shape[0], h), BF) for x, h in zip(grads, half)]
+    for _ in range(5):
+        scratch += [V((zc * r, h), BF) for r, h in zip(rows, half)]
+    scratch += [V((r, h), F32) for r, h in zip(rows, half)]
+    scratch += [V((r // 2, h), F32) for r, h in zip(rows, half)]
+    dma = pltpu.SemaphoreType.DMA
+    scratch += [V((n_dev,) + table.shape, F32), dma((n_dev,)), dma((n_dev,)), dma((count, 4)), dma((count, 4)), dma((count, 4)), dma((count, 3, zc)),
+                dma((count, zc)), dma((count, zc)), dma((count, zc)), dma((count, zc)), dma((count, zc)), dma((count, zc)), dma((count,)), dma((count,))]
+    return pl.pallas_call(
+        functools.partial(reduce_kernel, zc, count),
+        out_shape=outs,
+        in_specs=[pl.BlockSpec(memory_space=pl.ANY)] * count + [pl.BlockSpec(memory_space=pltpu.VMEM)],
+        out_specs=[pl.BlockSpec(memory_space=pltpu.VMEM)] * (count + 1),
+        scratch_shapes=scratch,
+        compiler_params=pltpu.CompilerParams(collective_id=1, has_side_effects=True, vmem_limit_bytes=48 << 20),
+        name="reduce_grads",
+    )(*grads, table)
+
+
+def two_level(q_weight, down_weight):
+    zc = lax.axis_size("wide") // 2
+    return (
+        lax.axis_size("dp") == 4
+        and lax.axis_size("wide") % 4 == 0
+        and q_weight.shape[0] % 8 == 0
+        and down_weight.shape[0] % 8 == 0
+    )
+
+
+def gathered(*weights):
+    q_w, k_w, v_w, o_w, gate_w, up_w, down_w, proj_w, g_a, g_f, g_e = weights
+    if not two_level(q_w, down_w):
+        return tuple(lax.all_gather(w, ("dp", "wide"), axis=0, tiled=True) for w in weights)
+    zc = lax.axis_size("wide") // 2
+    rows, width = q_w.shape
+    ff = gate_w.shape[1]
+    gains = jnp.pad(jnp.stack([g_a, g_f, g_e], axis=1), ((0, 0), (0, proj_w.shape[1] - 3)))
+    one = jnp.concatenate([q_w, k_w, v_w, o_w, proj_w, gains], axis=1)
+    two = jnp.concatenate([gate_w, up_w], axis=1)
+    spare = -rows % 16
+    one = jnp.pad(one, ((0, spare), (0, 0)))
+    two = jnp.pad(two, ((0, spare), (0, 0)))
+    one, two, down = gather([(one, rows), (two, rows), (down_w, down_w.shape[0])], zc, 8 * zc)
+    cuts = [one[:, i * width : (i + 1) * width] for i in range(4)]
+    last = one[:, 4 * width :]
+    p = proj_w.shape[1]
+    return (*cuts, two[:, :ff], two[:, ff:], down, last[:, :p], last[:, p], last[:, p + 1], last[:, p + 2])
+
+
+def scattered(grads, table):
+    q_g, k_g, v_g, o_g, gate_g, up_g, down_g, proj_g, a_g, f_g, e_g = grads
+    n_dev = lax.axis_size("dp") * lax.axis_size("wide")
+    rows = q_g.shape[0] // n_dev
+    if not two_level(q_g[:rows], down_g[: down_g.shape[0] // n_dev]):
+        shards = [lax.psum_scatter(g, ("dp", "wide"), scatter_dimension=0, tiled=True) for g in grads]
+        return (*shards, lax.psum(table, ("dp", "wide")))
+    zc = lax.axis_size("wide") // 2
+    width = q_g.shape[1]
+    p = proj_g.shape[1]
+    low = jnp.bfloat16
+    gains = jnp.pad(jnp.stack([a_g, f_g, e_g], axis=1), ((0, 0), (0, p - 3)))
+    one = jnp.concatenate([g.astype(low) for g in (q_g, k_g, v_g, o_g, proj_g, gains)], axis=1)
+    two = jnp.concatenate([gate_g.astype(low), up_g.astype(low)], axis=1)
+    flat = table.reshape(-1)
+    spare = -flat.shape[0] % 1024
+    packed = jnp.pad(flat, (0, spare)).reshape(-1, 128)
+    one, two, down, packed = reduce_scatter([one, two, down_g.astype(low)], packed, zc)
+    ff = gate_g.shape[1]
+    cuts = [one[:, i * width : (i + 1) * width] for i in range(4)]
+    last = one[:, 4 * width :]
+    return (
+        *cuts,
+        two[:, :ff],
+        two[:, ff:],
+        down,
+        last[:, :p],
+        last[:, p],
+        last[:, p + 1],
+        last[:, p + 2],
+        packed.reshape(-1)[: flat.shape[0]].reshape(table.shape),
+    )
 
 
 def cut_along(x, dim, length):
@@ -359,10 +822,10 @@
     final_gain,
     rel_bias,
 ):
-    micro_count = doc_tokens.shape[0]
-    doc_len = doc_tokens.shape[2]
-    slot_count = query_tokens.shape[2]
+    micro_count, _, doc_len, width = doc_tokens.shape
+    query_count, slot_count = query_tokens.shape[1:3]
     picks_width = retrieved.shape[3]
+    wide_count = lax.axis_size("wide")
     bias_table = rel_bias.astype(jnp.float32)
     onehot_doc = bucket_onehot(doc_len, rel_bias.shape[0])
     onehot_query = bucket_onehot(slot_count, rel_bias.shape[0])
@@ -371,95 +834,56 @@
     doc_valid = jnp.ones((1, doc_len), dtype=bool)
     slot_ids = jnp.arange(slot_count, dtype=jnp.int32)
     positions = lax.axis_index("wide") * doc_len + jnp.arange(doc_len, dtype=jnp.int32)
-    wide_count = lax.axis_size("wide")
+    full_weights = gathered(q_weight, k_weight, v_weight, o_weight, gate_weight, up_weight, down_weight, proj_weight, attn_gain, ffn_gain, final_gain)
     picks_group = lax.all_gather(retrieved, "wide", axis=1, tiled=True)
-    loss_list = []
-    doc_grad_list = []
-    query_grad_list = []
-    table_total = jnp.zeros(rel_bias.shape, jnp.float32)
-    for micro_step in range(micro_count):
-        full_weights = (
-            lax.all_gather(q_weight, ("dp", "wide"), axis=0, tiled=True),
-            lax.all_gather(k_weight, ("dp", "wide"), axis=0, tiled=True),
-            lax.all_gather(v_weight, ("dp", "wide"), axis=0, tiled=True),
-            lax.all_gather(o_weight, ("dp", "wide"), axis=0, tiled=True),
-            lax.all_gather(gate_weight, ("dp", "wide"), axis=0, tiled=True),
-            lax.all_gather(up_weight, ("dp", "wide"), axis=0, tiled=True),
-            lax.all_gather(down_weight, ("dp", "wide"), axis=0, tiled=True),
-            lax.all_gather(proj_weight, ("dp", "wide"), axis=0, tiled=True),
-            lax.all_gather(attn_gain, ("dp", "wide"), axis=0, tiled=True),
-            lax.all_gather(ffn_gain, ("dp", "wide"), axis=0, tiled=True),
-            lax.all_gather(final_gain, ("dp", "wide"), axis=0, tiled=True),
+    docs = doc_tokens.reshape(micro_count, doc_len, width)
+    queries = query_tokens.reshape(micro_count * query_count, slot_count, width)
+    query_valid = slot_ids[None, :] < query_lengths.reshape(-1)[:, None]
+    doc_emb, doc_state = encode_forward(docs, doc_valid, bias_doc, full_weights)
+    query_emb, query_state = encode_forward(queries, query_valid, bias_query, full_weights)
+    doc_emb = doc_emb.reshape(micro_count, doc_len, -1)
+    query_emb = query_emb.reshape(micro_count, query_count * slot_count, -1)
+    query_all = lax.all_gather(query_emb, "wide", axis=1, tiled=True)
+    pooled = jnp.stack([
+        score_forward(query_all[m], picks_group[m].reshape(-1, picks_width), doc_emb[m], positions)
+        for m in range(micro_count)
+    ])
+    pooled_query = lax.all_to_all(
+        pooled.reshape(micro_count, wide_count, -1), "wide", split_axis=1, concat_axis=1, tiled=True
+    )
+    results = [
+        query_loss(pooled_query[m], retrieved[m].reshape(-1, picks_width), query_lengths[m], targets[m], doc_len)
+        for m in range(micro_count)
+    ]
+    losses_out = jnp.stack([r[0] for r in results])
+    d_pooled = jnp.stack([r[1] for r in results])
+    d_pooled_doc = lax.all_to_all(d_pooled, "wide", split_axis=1, concat_axis=1, tiled=True)
+    backs = [
+        score_backward(
+            query_all[m],
+            picks_group[m].reshape(-1, picks_width),
+            doc_emb[m],
+            positions,
+            d_pooled_doc[m].reshape(-1),
         )
-        query_valid = slot_ids[None, :] < query_lengths[micro_step][:, None]
-        doc_emb, doc_state = encode_forward(
-            doc_tokens[micro_step], doc_valid, bias_doc, full_weights
-        )
-        query_emb, query_state = encode_forward(
-            query_tokens[micro_step], query_valid, bias_query, full_weights
-        )
-        query_all = lax.all_gather(query_emb, "wide", axis=0, tiled=True)
-        picks_all = picks_group[micro_step].reshape(-1, picks_width)
-        pooled = score_forward(query_all, picks_all, doc_emb, positions)
-        pooled_query = lax.all_to_all(
-            pooled.reshape(wide_count, -1), "wide", split_axis=0, concat_axis=0, tiled=True
-        )
-        own_picks = retrieved[micro_step].reshape(-1, picks_width)
-        losses, d_pooled = query_loss(
-            pooled_query, own_picks, query_lengths[micro_step], targets[micro_step], doc_len
-        )
-        d_pooled_doc = lax.all_to_all(d_pooled, "wide", split_axis=0, concat_axis=0, tiled=True)
-        doc_emb_grad, query_all_grad = score_backward(
-            query_all, picks_all, doc_emb, positions, d_pooled_doc.reshape(-1)
-        )
-        query_emb_grad = sent_and_summed(query_all_grad.astype(jnp.bfloat16), "wide", 0)
-        doc_in_grad, doc_weight_grads, doc_table = encode_backward(
-            doc_emb_grad, doc_state, doc_valid, bias_doc, onehot_doc, full_weights
-        )
-        query_in_grad, query_weight_grads, query_table = encode_backward(
-            query_emb_grad, query_state, query_valid, bias_query, onehot_query, full_weights
-        )
-        step_grads = jax.tree.map(jnp.add, doc_weight_grads, query_weight_grads)
-        table_total = table_total + doc_table + query_table
-        loss_list.append(losses)
-        doc_grad_list.append(doc_in_grad.reshape(doc_tokens.shape[1:]))
-        query_grad_list.append(query_in_grad.reshape(query_tokens.shape[1:]))
-        step_shards = (
-            lax.psum_scatter(step_grads[0], ("dp", "wide"), scatter_dimension=0, tiled=True),
-            lax.psum_scatter(step_grads[1], ("dp", "wide"), scatter_dimension=0, tiled=True),
-            lax.psum_scatter(step_grads[2], ("dp", "wide"), scatter_dimension=0, tiled=True),
-            lax.psum_scatter(step_grads[3], ("dp", "wide"), scatter_dimension=0, tiled=True),
-            lax.psum_scatter(step_grads[4], ("dp", "wide"), scatter_dimension=0, tiled=True),
-            lax.psum_scatter(step_grads[5], ("dp", "wide"), scatter_dimension=0, tiled=True),
-            lax.psum_scatter(step_grads[6], ("dp", "wide"), scatter_dimension=0, tiled=True),
-            lax.psum_scatter(step_grads[7], ("dp", "wide"), scatter_dimension=0, tiled=True),
-            lax.psum_scatter(step_grads[8], ("dp", "wide"), scatter_dimension=0, tiled=True),
-            lax.psum_scatter(step_grads[9], ("dp", "wide"), scatter_dimension=0, tiled=True),
-            lax.psum_scatter(step_grads[10], ("dp", "wide"), scatter_dimension=0, tiled=True),
-        )
-        shard_total = (
-            step_shards if micro_step == 0 else jax.tree.map(jnp.add, shard_total, step_shards)
-        )
-    table_grad = lax.psum(table_total, ("dp", "wide"))
-    losses_out = jnp.stack(loss_list)
-    doc_grad_out = jnp.stack(doc_grad_list)
-    query_grad_out = jnp.stack(query_grad_list)
+        for m in range(micro_count)
+    ]
+    doc_emb_grad = jnp.concatenate([b[0] for b in backs])
+    query_all_grad = jnp.stack([b[1] for b in backs])
+    query_emb_grad = sent_and_summed(query_all_grad.astype(jnp.bfloat16), "wide", 1)
+    doc_in_grad, doc_grads, doc_table = encode_backward(
+        doc_emb_grad, doc_state, doc_valid, bias_doc, onehot_doc, full_weights
+    )
+    query_in_grad, query_grads, query_table = encode_backward(
+        query_emb_grad.reshape(-1, query_emb_grad.shape[-1]), query_state, query_valid, bias_query, onehot_query, full_weights
+    )
+    grads = jax.tree.map(jnp.add, doc_grads, query_grads)
+    shards = scattered(grads, doc_table + query_table)
     return (
         losses_out,
-        doc_grad_out,
-        query_grad_out,
-        shard_total[0],
-        shard_total[1],
-        shard_total[2],
-        shard_total[3],
-        shard_total[4],
-        shard_total[5],
-        shard_total[6],
-        shard_total[7],
-        shard_total[8],
-        shard_total[9],
-        shard_total[10],
-        table_grad,
+        doc_in_grad.reshape(doc_tokens.shape),
+        query_in_grad.reshape(query_tokens.shape),
+        *shards,
     )
 
 

time: 1580 us -> 782 us (0.49)
  waiting for transfers between devices: 774 us -> 4.15 us
  Pallas kernels: 0 us -> 189 us
  blocking collectives: 163 us -> 30.6 us
  matrix products: 337 us -> 281 us
  other arithmetic: 90.9 us -> 117 us
  local copies, waits for them, and re-layouts: 153 us -> 133 us
    reduce_scatter x7 -> x0, waiting for transfers between devices: 609 us -> none  [the longest x1 121 us: local(): lax.psum_scatter(step_grads[6], ('dp', 'wide'), scatter_dimension=0, tile...]
    pallas_call x0 -> x2, Pallas kernels: none -> 189 us  [the longest x1 109 us: reduce_scatter(): pl.pallas_call(functools.partial(reduce_kernel, zc, count), out_shape=out...]
    all_gather x7 -> x0, waiting for transfers between devices: 150 us -> none  [the longest x1 58.3 us: local(): lax.all_gather(up_weight, ('dp', 'wide'), axis=0, tiled=True)]
    unnamed x2 -> x0, blocking collectives: 75.7 us -> none
    all_gather x3 -> x1, blocking collectives: 71 us -> 15.7 us  [local(): query_all = lax.all_gather(query_emb, 'wide', axis=1, tiled=True)]
    mul x2 -> x0, local copies, waits for them, and re-layouts: 37.9 us -> none  [encode_backward(): probs_attn * (d_probs - jnp.sum(probs_attn * d_probs, axis=-1, keepdims=T...]
    reduce_sum x2, other arithmetic: 2.61 us -> 33.3 us  [encode_backward(): jnp.sum(d_scores, axis=0)]
    dot_general x34 -> x18, matrix products: 75.1 us -> 46.8 us  [contract_rows(): lax.dot_general(left_mat, right_mat, (((0,), (0,)), ((), ())), preferred_...]
  transfers between devices with their start and end apart: 21 -> 3, of which waited for: 15 -> 1; matrix products, arithmetic and copies ran while one was open for 27% -> 10% of each run, Pallas kernels for 0% -> 0%
where the time goes in v1:
time: 782 us; the launch traced here: 772 us
  matrix products  281 us (36%)
  Pallas kernels  189 us (24%)
  local copies, waits for them, and re-layouts  133 us (17%)
  other arithmetic  117 us (15%)
  blocking collectives  30.6 us (4%)
  starting transfers between devices  14.1 us (2%)
    pallas_call x1, Pallas kernels, reduce_scatter(): pl.pallas_call(functools.partial(reduce_kernel, zc, count), out_shape=out...  109 us
    pallas_call x1, Pallas kernels, gather(): pl.pallas_call(functools.partial(gather_kernel, zc, count), out_shape=out...  79.3 us
    dot_general x18, matrix products, contract_cols(): lax.dot_general(left_mat, right_mat, (((1,), (1,)), ((), ())), preferred_...  70.3 us
    dot_general x18, matrix products, contract_rows(): lax.dot_general(left_mat, right_mat, (((0,), (0,)), ((), ())), preferred_...  46.8 us
    dot_general x18, matrix products, matmul(): return jnp.dot(left_mat, right_mat, preferred_element_type=jnp.float32)  42.9 us
    reduce_sum x2, other arithmetic, encode_backward(): jnp.sum(d_scores, axis=0)  33.3 us
    dot_general x2, matrix products, encode_backward(): jnp.einsum('bqhd,bkhd->bhqk', d_context, values_h, preferred_element_type...  23.8 us
    dot_general x2, matrix products, encode_backward(): jnp.einsum('hij,ijb->bh', jnp.sum(d_scores, axis=0), onehot_table, precis...  23.1 us
  transfers between devices with their start and end apart: 3, of which 1 were waited for; matrix products, arithmetic and copies ran while one was open for 10% of the time, Pallas kernels for 0%

profile of v1, /device:TPU:1, one launch (start us, length us, event | category | flops | bytes accessed | tf_op | source)
XLA Modules:
  0.0 771.6 jit_solution(8127583793676654134)
XLA Ops:
  11.3 79.3 %gather_weights.1 = (bf16[768,3328]{1,0:T(8,128)(2,1)S(1)}, bf16[768,4096]{1,0:T(8,128)(2,1)S(1)}, bf16[2048,768]{1,0:T(8,128)(2,1)S(1)}) custom-call(bf16[32,3328]{1,0:T(8,128)(2,1)S(1)} %pad.22.refs_0_, bf16[32,4096]{1,0:T(8,128)(2,1)S(1)} %fusion.176.refs_1_, bf16[64,768]{1,0:T(8,128)(2,1)S(1)} %copy-done.4), custom_call_target="tpu_custom_call" | custom-call | tf_op jit(solution)/shard_map/gather_weights/pallas_call | solution.py:183
  109.9 14.9 %all_gather.6 = s32[2,16,32,32]{3,2,1,0:T(8,128)S(1)} all-gather(s32[2,2,32,32]{3,2,1,0:T(8,128)S(1)} %copy-done.89), channel_id=1, replica_groups=mesh['dp'=4,'wide'=8] {'wide'}, dimensions={1}, use_global_device_ids=true | all-gather | bytes 147456 | tf_op jit(solution)/shard_map/all_gather | solution.py:838
  124.9 20.2 %convert_reduce_fusion.2 = (f32[512]{0:T(512)}, f32[512,512]{1,0:T(8,128)}, f32[512,512]{1,0:T(8,128)}, f32[512]{0:T(512)}) fusion(s32[512]{0:T(512)S(1)} %iota_add_fusion, s32[512,32]{1,0:T(8,128)S(1)} %bitcast.294, s32[512,32]{1,0:T(8,128)S(1)} %bitcast.293), kind=kLoop, calls=%fused_computation.2 | loop fusion | flops 66583552 | bytes 2234368 | tf_op jit(solution)/shard_map/while/body/eval_jaxpr/reduce_sum | solution.py:724
  194.3 15.7 %all_gather.7 = bf16[2,512,128]{2,1,0:T(8,128)(2,1)} all-gather(bf16[2,64,128]{2,1,0:T(8,128)(2,1)S(1)} %bitcast.300), channel_id=1, replica_groups=mesh['dp'=4,'wide'=8] {'wide'}, dimensions={1}, use_global_device_ids=true | all-gather | bytes 294912 | tf_op jit(solution)/shard_map/all_gather | solution.py:846
  210.1 8.5 %fusion.11 = f32[12,512,512]{2,0,1:T(8,128)} fusion(s32[512,512]{1,0:T(8,128)S(1)} %copy-done.16, bf16[32,12]{0,1:T(8,128)(2,1)S(1)} %copy-done), kind=kOutput, calls=%fused_computation.23 | convolution fusion | flops 209715200 | bytes 13632256 | tf_op jit(solution)/shard_map/ijb,bh->hij/dot_general | solution.py:832
  218.5 17.8 %copy.193 = f32[12,512,512]{1,2,0:T(8,128)} copy(f32[12,512,512]{2,0,1:T(8,128)} %fusion.11) | data formatting | bytes 25165824 | tf_op jit(solution)/shard_map/ijb,bh->hij/dot_general | solution.py:832
  236.3 13.7 %add_reduce_fusion = (f32[2,12,512]{2,1,0:T(8,128)S(1)}, f32[2,12,512,512]{2,3,1,0:T(8,128)}) fusion(f32[12,512,512]{1,2,0:T(8,128)} %copy.193, bf16[2,512,12,64]{1,0,3,2:T(2,128)(2,1)} %reshape.959, bf16[2,512,12,64]{1,0,3,2:T(2,128)(2,1)} %reshape.958), kind=kOutput, calls=%fused_computation.13 | convolution fusion | flops 817876992 | bytes 40943616 | tf_op jit(solution)/shard_map/bqhd,bkhd->bhqk/dot_general | solution.py:531
  250.0 13.1 %fusion.2 = f32[2,12,512]{2,1,0:T(8,128)S(1)} fusion(f32[2,12,512,512]{2,3,1,0:T(8,128)} %get-tuple-element.248, f32[2,12,512]{2,1,0:T(8,128)S(1)} %get-tuple-element.247, f32[12,512,512]{1,2,0:T(8,128)} %copy.193), kind=kLoop, calls=%fused_computation.12 | loop fusion | flops 18862080 | bytes 37847040 | tf_op jit(solution)/shard_map/reduce_sum | solution.py:568
  263.2 16.2 %fusion.78 = bf16[2,512,12,64]{1,3,2,0:T(8,128)(2,1)} fusion(f32[2,12,512,512]{2,3,1,0:T(8,128)} %get-tuple-element.248, f32[2,12,512]{2,1,0:T(8,128)S(1)} %fusion.2, f32[2,12,512]{2,1,0:T(8,128)S(1)} %get-tuple-element.247, f32[12,512,512]{1,2,0:T(8,128)} %copy.193, bf16[2,512,12,64]{1,0,3,2:T(2,128)(2,1)} %reshape.957), kind=kOutput, calls=%fused_computation.112 | convolution fusion | flops 831258624 | bytes 40992768 | tf_op jit(solution)/shard_map/bhqk,bkhd->bqhd/dot_general | solution.py:571
  290.4 7.1 multiply_convert_fusion.1
  346.5 5.6 all-to-all-start.1
  372.1 13.8 %fusion.18 = (bf16[1024,2048]{1,0:T(8,128)(2,1)}, bf16[1024,2048]{1,0:T(8,128)(2,1)}) fusion(f32[1024,2048]{1,0:T(8,128)} %copy-done.123, f32[1024,2048]{1,0:T(8,128)} %get-tuple-element.252, bf16[2048,768]{1,0:T(8,128)(2,1)S(1)} %get-tuple-element.100, f32[1024,768]{1,0:T(8,128)S(1)} %multiply_subtract_fusion), kind=kOutput, calls=%fused_computation.30 | convolution fusion | flops 3272343552 | bytes 31457280 | tf_op jit(solution)/shard_map/dot_general | solution.py:495
  397.1 5.6 fusion.240
  420.0 15.8 %fusion.69 = bf16[2,512,12,64]{1,3,2,0:T(8,128)(2,1)} fusion(f32[2,12,512,512]{2,3,1,0:T(8,128)} %get-tuple-element.248, f32[2,12,512]{2,1,0:T(8,128)S(1)} %log_add_fusion, f32[12,512,512]{1,2,0:T(8,128)} %copy.193, bf16[2,512,12,64]{1,0,3,2:T(2,128)(2,1)} %reshape.961), kind=kOutput, calls=%fused_computation.109 | convolution fusion | flops 824967168 | bytes 40943616 | tf_op jit(solution)/shard_map/bhqk,bqhd->bkhd/dot_general | solution.py:672
  435.8 22.3 %multiply_reduce_fusion = (f32[2,12,512]{2,1,0:T(8,128)S(1)}, f32[2,12,512,512]{2,3,1,0:T(8,128)}) fusion(f32[2,12,512,512]{2,3,1,0:T(8,128)} %get-tuple-element.248, f32[2,12,512]{2,1,0:T(8,128)S(1)} %log_add_fusion, f32[12,512,512]{1,2,0:T(8,128)} %copy.193, bf16[2,512,12,64]{1,0,3,2:T(2,128)(2,1)} %reshape.957, bf16[2,512,12,64]{1,0,3,2:T(2,128)(2,1)} %reshape.961), kind=kOutput, calls=%fused_computation.8 | convolution fusion | flops 830459904 | bytes 66158592 | tf_op jit(solution)/shard_map/bqhd,bkhd->bhqk/dot_general | solution.py:671
  458.1 31.6 %fusion.227 = (f32[12,512,512]{1,2,0:T(8,128)}, bf16[2,12,512,512]{2,3,1,0:T(8,128)(2,1)}) fusion(f32[2,12,512,512]{2,3,1,0:T(8,128)} %get-tuple-element.262, f32[2,12,512]{2,1,0:T(8,128)S(1)} %get-tuple-element.261, f32[2,12,512]{2,1,0:T(8,128)S(1)} %log_add_fusion, f32[2,12,512,512]{2,3,1,0:T(8,128)} %get-tuple-element.248, f32[12,512,512]{1,2,0:T(8,128)} %copy.193), kind=kLoop, calls=%fused_computation.402 | loop fusion | flops 34603008 | bytes 88178688 | tf_op jit(solution)/shard_map/reduce_sum | solution.py:681
  489.7 8.6 %fusion.72 = bf16[2,512,12,64]{1,3,2,0:T(8,128)(2,1)S(1)} fusion(bf16[2,12,512,512]{2,3,1,0:T(8,128)(2,1)} %get-tuple-element.212, bf16[2,512,12,64]{1,0,3,2:T(2,128)(2,1)S(1)} %copy-done.17), kind=kOutput, calls=%fused_computation.110 | convolution fusion | flops 806092800 | bytes 15728640 | tf_op jit(solution)/shard_map/bhqk,bqhd->bkhd/dot_general | solution.py:688
  498.3 6.5 fusion.75
  536.7 5.8 fusion.35
  542.6 18.5 %copy.237 = f32[12,512,512]{2,0,1:T(8,128)} copy(f32[12,512,512]{1,2,0:T(8,128)} %get-tuple-element.211) | data formatting | bytes 25165824 | tf_op jit(solution)/shard_map/reduce_sum | solution.py:681
  561.0 21.1 %fusion.101 = f32[32,12]{0,1:T(8,128)} fusion(f32[12,512,512]{2,0,1:T(8,128)} %copy.237, s32[512,512]{1,0:T(8,128)} %fusion.110), kind=kOutput, calls=%fused_computation.156 | convolution fusion | flops 1216348160 | bytes 13633024 | tf_op jit(solution)/shard_map/hij,ijb->bh/dot_general | solution.py:680
  624.5 5.7 add_convert_fusion.1
  641.6 6.3 pad_maximum_fusion.refs_1_
  655.6 109.2 %reduce_grads.1 = (f32[24,3328]{1,0:T(8,128)S(1)}, f32[24,4096]{1,0:T(8,128)S(1)}, f32[64,768]{1,0:T(8,128)S(1)}, f32[8,128]{1,0:T(8,128)S(1)}) custom-call(bf16[768,3328]{1,0:T(8,128)(2,1)} %copy-done.29, bf16[768,4096]{1,0:T(8,128)(2,1)} %pad_maximum_fusion.refs_1_, bf16[2048,768]{1,0:T(8,128)(2,1)S(1)} %add_convert_fusion.refs_2_, ...), custom_call_target="tpu_custom_call" | custom-call | tf_op jit(solution)/shard_map/reduce_grads/pallas_call | solution.py:401
  (491 shorter events, 285.8 us)
Async XLA Ops:
  0.6 107.9 %copy-start = (bf16[32,12]{0,1:T(8,128)(2,1)S(1)}, bf16[32,12]{0,1:T(8,128)(2,1)}, u32[]{:S(2)}) copy-start(bf16[32,12]{0,1:T(8,128)(2,1)} %param.33) | copy-start | bytes 2308
  0.7 93.0 %copy-start.40 = (bf16[2,2,32,768]{3,2,1,0:T(8,128)(2,1)S(1)}, bf16[2,2,32,768]{3,2,1,0:T(8,128)(2,1)}, u32[]{:S(2)}) copy-start(bf16[2,2,32,768]{3,2,1,0:T(8,128)(2,1)} %param.18) | copy-start | bytes 589828
  93.7 241.5 %copy-start.87 = (f32[768]{0:T(1024)}, f32[768]{0:T(1024)S(1)}, u32[]{:S(2)}) copy-start(f32[768]{0:T(1024)S(1)} %get-tuple-element.179) | copy-start | bytes 9220
  93.7 270.8 %copy-start.85 = (f32[768]{0:T(1024)}, f32[768]{0:T(1024)S(1)}, u32[]{:S(2)}) copy-start(f32[768]{0:T(1024)S(1)} %get-tuple-element.177) | copy-start | bytes 9220
  164.2 27.5 %copy-start.36 = (f32[128,768]{1,0:T(8,128)}, f32[128,768]{1,0:T(8,128)S(1)}, u32[]{:S(2)}) copy-start(f32[128,768]{1,0:T(8,128)S(1)} %get-tuple-element.242) | copy-start | bytes 1179652
  301.6 22.0 %copy-start.41 = (bf16[2,2,32,768]{3,2,1,0:T(8,128)(2,1)S(1)}, bf16[2,2,32,768]{3,2,1,0:T(8,128)(2,1)}, u32[]{:S(2)}) copy-start(bf16[2,2,32,768]{3,2,1,0:T(8,128)(2,1)} %param.18) | copy-start | bytes 589828
  304.4 20.5 %copy-start.83 = (f32[4,12,32]{2,1,0:T(8,128)S(1)}, f32[4,12,32]{2,1,0:T(8,128)}, u32[]{:S(2)}) copy-start(f32[4,12,32]{2,1,0:T(8,128)} %copy-done.82) | copy-start | bytes 18436
  304.5 20.5 %copy-start.93 = (f32[4,12,32]{2,1,0:T(8,128)S(1)}, f32[4,12,32]{2,1,0:T(8,128)}, u32[]{:S(2)}) copy-start(f32[4,12,32]{2,1,0:T(8,128)} %copy-done.92) | copy-start | bytes 18436
  316.9 22.0 %all-to-all-start = ((f32[8,1,128]{2,1,0:T(1,128)}), f32[8,1,128]{2,1,0:T(1,128)}, u32[]{:S(2)}, u32[]{:S(2)}) async-start(f32[8,1,128]{2,1,0:T(1,128)} %reshape.1010), calls=%async_computation | async-start | bytes 8192 | tf_op jit(solution)/shard_map/all_to_all | solution.py:851
  325.6 32.1 %copy-start.99 = (f32[512]{0:T(512)S(1)}, f32[512]{0:T(512)}, u32[]{:S(2)}) copy-start(f32[512]{0:T(512)} %get-tuple-element.191) | copy-start | bytes 6148
  325.6 32.1 %copy-start.101 = (f32[512]{0:T(512)S(1)}, f32[512]{0:T(512)}, u32[]{:S(2)}) copy-start(f32[512]{0:T(512)} %get-tuple-element.204) | copy-start | bytes 6148
  325.6 32.1 %copy-start.103 = (f32[512]{0:T(512)S(1)}, f32[512]{0:T(512)}, u32[]{:S(2)}) copy-start(f32[512]{0:T(512)} %copy-done.102) | copy-start | bytes 6148
  325.6 32.1 %copy-start.105 = (f32[512]{0:T(512)S(1)}, f32[512]{0:T(512)}, u32[]{:S(2)}) copy-start(f32[512]{0:T(512)} %copy-done.104) | copy-start | bytes 6148
  334.3 25.5 %copy-start.54 = (bf16[2,512,128]{2,1,0:T(8,128)(2,1)S(1)}, bf16[2,512,128]{2,1,0:T(8,128)(2,1)}, u32[]{:S(2)}) copy-start(bf16[2,512,128]{2,1,0:T(8,128)(2,1)} %all_gather.7) | copy-start | bytes 786436
  346.5 10.3 %all-to-all-start.1 = ((f32[8,1,128]{2,1,0:T(1,128)}), f32[8,1,128]{2,1,0:T(1,128)S(1)}, u32[]{:S(2)}, u32[]{:S(2)}) async-start(f32[8,1,128]{2,1,0:T(1,128)} %reshape.1012), calls=%async_computation.1 | async-start | bytes 8192 | tf_op jit(solution)/shard_map/all_to_all | solution.py:860
  366.7 19.3 %slice-start.2 = ((s8[6291456]{0:T(1024)(128)(4,1)}), s8[4194304]{0:T(1024)(128)(4,1)S(1)}, s32[]{:S(2)}) async-start(s8[6291456]{0:T(1024)(128)(4,1)} %bitcast.269), calls=%async_computation.5 | async-start | bytes 8388608
  458.1 31.6 %copy-start.17 = (bf16[2,512,12,64]{1,0,3,2:T(2,128)(2,1)S(1)}, bf16[2,512,12,64]{1,0,3,2:T(2,128)(2,1)}, u32[]{:S(2)}) copy-start(bf16[2,512,12,64]{1,0,3,2:T(2,128)(2,1)} %reshape.958) | copy-start | bytes 4718596
  524.6 64.5 %all-to-all-start.2 = ((bf16[8,2,64,128]{3,2,1,0:T(8,128)(2,1)}), bf16[8,2,64,128]{3,2,1,0:T(8,128)(2,1)}, u32[]{:S(2)}, u32[]{:S(2)}) async-start(bf16[8,2,64,128]{3,2,1,0:T(8,128)(2,1)} %maximum_bitcast_fusion), calls=%async_computation.2 | async-start | bytes 524288 | tf_op jit(solution)/shard_map/all_to_all | solution.py:484
  561.0 21.1 %copy-start.8 = (bf16[2,1,512,768]{3,2,1,0:T(8,128)(2,1)S(1)}, bf16[2,1,512,768]{3,2,1,0:T(8,128)(2,1)}, u32[]{:S(2)}) copy-start(bf16[2,1,512,768]{3,2,1,0:T(8,128)(2,1)} %param.17) | copy-start | bytes 4718596
  561.0 21.1 %copy-start.23 = (f32[1024,768]{1,0:T(8,128)S(1)}, f32[1024,768]{1,0:T(8,128)}, u32[]{:S(2)}) copy-start(f32[1024,768]{1,0:T(8,128)} %copy-done.22) | copy-start | bytes 9437188
  561.0 21.1 %copy-start.24 = (f32[1024,768]{1,0:T(8,128)S(1)}, f32[1024,768]{1,0:T(8,128)}, u32[]{:S(2)}) copy-start(f32[1024,768]{1,0:T(8,128)} %get-tuple-element.267) | copy-start | bytes 9437188
  655.6 111.2 %copy-start.122 = (f32[128]{0:T(128)S(1)}, f32[128]{0:T(128)}, u32[]{:S(2)}) copy-start(f32[128]{0:T(128)} %get-tuple-element.187) | copy-start | bytes 1540
  655.6 112.8 %copy-start.43 = (bf16[2,2,32,768]{3,2,1,0:T(8,128)(2,1)S(1)}, bf16[2,2,32,768]{3,2,1,0:T(8,128)(2,1)}, u32[]{:S(2)}) copy-start(bf16[2,2,32,768]{3,2,1,0:T(8,128)(2,1)} %param.18) | copy-start | bytes 589828
  655.6 115.5 %copy-start.1 = (bf16[32,12]{0,1:T(8,128)(2,1)S(1)}, bf16[32,12]{0,1:T(8,128)(2,1)}, u32[]{:S(2)}) copy-start(bf16[32,12]{0,1:T(8,128)(2,1)} %param.33) | copy-start | bytes 2308
  (111 other events, 474.8 us)

commit v2 on v1

--- a/solution.py
+++ b/solution.py
@@ -11,7 +11,8 @@
 score_scale = 6.0
 mask_fill = -1000000000.0
 top_precision = lax.Precision.HIGHEST
-block_rows = 512
+F32 = jnp.float32
+BF = jnp.bfloat16
 
 
 MESH = pl.DeviceIdType.MESH
@@ -190,8 +191,6 @@
         name="gather_weights",
     )(*[s for s, _ in shards])
 
-
-F32 = jnp.float32; BF = jnp.bfloat16
 
 def reduce_kernel(zc, count, *refs):
     pos = Place(zc)
@@ -409,80 +408,325 @@
     )(*grads, table)
 
 
-def two_level(q_weight, down_weight):
-    zc = lax.axis_size("wide") // 2
-    return (
-        lax.axis_size("dp") == 4
-        and lax.axis_size("wide") % 4 == 0
-        and q_weight.shape[0] % 8 == 0
-        and down_weight.shape[0] % 8 == 0
-    )
-
-
-def gathered(*weights):
-    q_w, k_w, v_w, o_w, gate_w, up_w, down_w, proj_w, g_a, g_f, g_e = weights
-    if not two_level(q_w, down_w):
-        return tuple(lax.all_gather(w, ("dp", "wide"), axis=0, tiled=True) for w in weights)
-    zc = lax.axis_size("wide") // 2
-    rows, width = q_w.shape
-    ff = gate_w.shape[1]
-    gains = jnp.pad(jnp.stack([g_a, g_f, g_e], axis=1), ((0, 0), (0, proj_w.shape[1] - 3)))
-    one = jnp.concatenate([q_w, k_w, v_w, o_w, proj_w, gains], axis=1)
-    two = jnp.concatenate([gate_w, up_w], axis=1)
-    spare = -rows % 16
-    one = jnp.pad(one, ((0, spare), (0, 0)))
-    two = jnp.pad(two, ((0, spare), (0, 0)))
-    one, two, down = gather([(one, rows), (two, rows), (down_w, down_w.shape[0])], zc, 8 * zc)
-    cuts = [one[:, i * width : (i + 1) * width] for i in range(4)]
-    last = one[:, 4 * width :]
-    p = proj_w.shape[1]
-    return (*cuts, two[:, :ff], two[:, ff:], down, last[:, :p], last[:, p], last[:, p + 1], last[:, p + 2])
-
-
-def scattered(grads, table):
-    q_g, k_g, v_g, o_g, gate_g, up_g, down_g, proj_g, a_g, f_g, e_g = grads
-    n_dev = lax.axis_size("dp") * lax.axis_size("wide")
-    rows = q_g.shape[0] // n_dev
-    if not two_level(q_g[:rows], down_g[: down_g.shape[0] // n_dev]):
-        shards = [lax.psum_scatter(g, ("dp", "wide"), scatter_dimension=0, tiled=True) for g in grads]
-        return (*shards, lax.psum(table, ("dp", "wide")))
-    zc = lax.axis_size("wide") // 2
-    width = q_g.shape[1]
-    p = proj_g.shape[1]
-    low = jnp.bfloat16
-    gains = jnp.pad(jnp.stack([a_g, f_g, e_g], axis=1), ((0, 0), (0, p - 3)))
-    one = jnp.concatenate([g.astype(low) for g in (q_g, k_g, v_g, o_g, proj_g, gains)], axis=1)
-    two = jnp.concatenate([gate_g.astype(low), up_g.astype(low)], axis=1)
-    flat = table.reshape(-1)
-    spare = -flat.shape[0] % 1024
-    packed = jnp.pad(flat, (0, spare)).reshape(-1, 128)
-    one, two, down, packed = reduce_scatter([one, two, down_g.astype(low)], packed, zc)
-    ff = gate_g.shape[1]
-    cuts = [one[:, i * width : (i + 1) * width] for i in range(4)]
-    last = one[:, 4 * width :]
-    return (
-        *cuts,
-        two[:, :ff],
-        two[:, ff:],
-        down,
-        last[:, :p],
-        last[:, p],
-        last[:, p + 1],
-        last[:, p + 2],
-        packed.reshape(-1)[: flat.shape[0]].reshape(table.shape),
-    )
-
-
-def cut_along(x, dim, length):
-    shape = x.shape
-    tiles = x.reshape(*shape[:dim], length, shape[dim] // length, *shape[dim + 1 :])
-    return jnp.moveaxis(tiles, dim, 0)
-
-
-def sent_and_summed(x, axis, dim):
-    length = lax.axis_size(axis)
-    tiles = lax.all_to_all(cut_along(x, dim, length), axis, 0, 0, tiled=True)
-    return jnp.sum(tiles.astype(jnp.float32), axis=0)
+def bucket_of(n):
+    far = jnp.zeros_like(n)
+    dist = jnp.abs(n)
+    for power_step in range(1, 8):
+        far = far + (dist * dist >= 64 * 2**power_step).astype(jnp.int32)
+    return jnp.where(n > 0, 16, 0) + jnp.where(dist < 8, dist, 8 + far)
+
+def diagonal_onehot(doc_len, bucket_count):
+    span = 2 * doc_len
+    i = jnp.arange(span, dtype=jnp.int32)
+    base = doc_len - 128
+    n = base - jnp.where(i >= span - 127, i - span, i)
+    inside = (n > -doc_len) & (n < doc_len)
+    hot = (bucket_of(n)[:, None] == jnp.arange(bucket_count, dtype=jnp.int32)[None, :]) & inside[:, None]
+    return hot.astype(F32)
+
+def cols_dot(a, b):
+    return lax.dot_general(a, b, (((1,), (1,)), ((), ())), preferred_element_type=F32)
+
+def tiles_of(table, keys, q_from, q_len, doc_len):
+    parts = []
+    for kb in range(keys // 128):
+        at = doc_len - 128 - 128 * kb + q_from
+        parts.append(table[:, at : at + q_len])
+    return jnp.concatenate(parts, axis=0) if len(parts) > 1 else parts[0]
+
+def attend_kernel(doc_len, doc_count, block, qkv_ref, diag_ref, mask_ref, ctx_ref, lse_ref, table_ref):
+    span = 2 * doc_len
+    hd = 64
+    for h in range(2):
+        wide = jnp.broadcast_to(diag_ref[0, h : h + 1, :], (128, span))
+        table_ref[h] = pltpu.roll(wide, 0, 1, stride=1, stride_axis=0)[:, : span - 128]
+    lane = lax.broadcasted_iota(jnp.int32, (1, 128), 1)
+    def part(rows, keys_from, keys, q_at, q_len, mask):
+        q2 = qkv_ref[pl.ds(rows + q_at, q_len), 0:128]
+        k2 = qkv_ref[pl.ds(rows + keys_from, keys), 128:256]
+        v2 = qkv_ref[pl.ds(rows + keys_from, keys), 256:384]
+        v2t = v2.astype(F32).T.astype(BF)
+        outs = []
+        for h in range(2):
+            qm = jnp.where((lane < hd) == (h == 0), q2, jnp.zeros_like(q2))
+            s = cols_dot(k2, qm) + tiles_of(table_ref.at[h], keys, q_at, q_len, doc_len)
+            if mask is not None:
+                s = jnp.where(mask > 0, s, mask_fill)
+            top = jnp.max(s, axis=0, keepdims=True)
+            e = jnp.exp(s - top)
+            total = jnp.sum(e, axis=0, keepdims=True)
+            p = (e * (1.0 / total)).astype(BF)
+            lse_ref[0, h : h + 1, pl.ds(rows + q_at, q_len)] = top + jnp.log(total)
+            outs.append(jnp.dot(v2t[h * hd : (h + 1) * hd], p, preferred_element_type=F32))
+        ctx_ref[pl.ds(rows + q_at, q_len), :] = jnp.concatenate(outs, axis=0).T.astype(BF)
+    for m in range(doc_count):
+        for q_at in range(0, doc_len, block):
+            part(m * doc_len, 0, doc_len, q_at, block, None)
+    rest = qkv_ref.shape[0] - doc_count * doc_len
+    for i in range(rest // 128):
+        part(doc_count * doc_len + 128 * i, 0, 128, 0, 128, mask_ref[i])
+
+def attend(qkv, diag, mask, doc_len, doc_count):
+    total, width = qkv.shape
+    pairs = width // 384
+    span = 2 * doc_len
+    return pl.pallas_call(
+        functools.partial(attend_kernel, doc_len, doc_count, 256),
+        grid=(pairs,),
+        in_specs=[
+            pl.BlockSpec((total, 384), lambda j: (0, j)),
+            pl.BlockSpec((1, 8, span), lambda j: (j, 0, 0)),
+            pl.BlockSpec(mask.shape, lambda j: (0, 0, 0)),
+        ],
+        out_specs=[
+            pl.BlockSpec((total, 128), lambda j: (0, j)),
+            pl.BlockSpec((1, 8, total), lambda j: (j, 0, 0)),
+            pl.BlockSpec((2, 128, span - 128), lambda j: (j, 0, 0)),
+        ],
+        out_shape=[
+            jax.ShapeDtypeStruct((total, pairs * 128), BF),
+            jax.ShapeDtypeStruct((pairs, 8, total), F32),
+            jax.ShapeDtypeStruct((pairs * 2, 128, span - 128), F32),
+        ],
+        compiler_params=pltpu.CompilerParams(vmem_limit_bytes=40 << 20),
+        name="attend",
+    )(qkv, diag, mask)
+
+def attend_back_kernel(doc_len, doc_count, block, qkv_ref, do_ref, lse_ref, table_ref, mask_ref, dqkv_ref, diag_ref, acc):
+    span = 2 * doc_len
+    hd = 64
+    acc[...] = jnp.zeros_like(acc)
+    lane = lax.broadcasted_iota(jnp.int32, (1, 128), 1)
+    def part(rows, keys, q_len, mask):
+        k2 = qkv_ref[pl.ds(rows, keys), 128:256]
+        v2 = qkv_ref[pl.ds(rows, keys), 256:384]
+        k2t = k2.astype(F32).T.astype(BF)
+        dk = jnp.zeros((keys, 128), F32)
+        dv = jnp.zeros((keys, 128), F32)
+        for q_at in range(0, keys, q_len):
+            qr = pl.ds(rows + q_at, q_len)
+            q2 = qkv_ref[qr, 0:128]
+            do2 = do_ref[qr, :]
+            outs = []
+            for h in range(2):
+                mine = (lane < hd) == (h == 0)
+                qm = jnp.where(mine, q2, jnp.zeros_like(q2))
+                dom = jnp.where(mine, do2, jnp.zeros_like(do2))
+                s = cols_dot(k2, qm) + tiles_of(table_ref.at[h], keys, q_at, q_len, doc_len)
+                if mask is not None:
+                    s = jnp.where(mask > 0, s, mask_fill)
+                p = jnp.exp(s - lse_ref[0, h : h + 1, qr])
+                dp = cols_dot(v2, dom)
+                ds = p * (dp - jnp.sum(p * dp, axis=0, keepdims=True))
+                for kb in range(keys // 128):
+                    at = doc_len - 128 - 128 * kb + q_at
+                    acc[h, :, at : at + q_len] += ds[128 * kb : 128 * (kb + 1)]
+                low = ds.astype(BF)
+                dv += jnp.dot(p.astype(BF), dom, preferred_element_type=F32)
+                dk += jnp.dot(low, qm, preferred_element_type=F32)
+                outs.append(jnp.dot(k2t[h * hd : (h + 1) * hd], low, preferred_element_type=F32))
+            dqkv_ref[qr, 0:128] = jnp.concatenate(outs, axis=0).T.astype(BF)
+        dqkv_ref[pl.ds(rows, keys), 128:256] = dk.astype(BF)
+        dqkv_ref[pl.ds(rows, keys), 256:384] = dv.astype(BF)
+    for m in range(doc_count):
+        part(m * doc_len, doc_len, block, None)
+    rest = qkv_ref.shape[0] - doc_count * doc_len
+    for i in range(rest // 128):
+        part(doc_count * doc_len + 128 * i, 128, 128, mask_ref[i])
+    for h in range(2):
+        eight = acc[h, 0:8]
+        for g in range(1, 16):
+            eight = eight + pltpu.roll(acc[h, 8 * g : 8 * g + 8], span - 8 * g, 1)
+        one = eight[0:1]
+        for r in range(1, 8):
+            one = one + pltpu.roll(eight, span - r, 1)[r : r + 1]
+        diag_ref[0, h : h + 1, :] = one
+
+def attend_back(qkv, d_ctx, lse, table, mask, doc_len, doc_count):
+    total, width = qkv.shape
+    pairs = width // 384
+    span = 2 * doc_len
+    return pl.pallas_call(
+        functools.partial(attend_back_kernel, doc_len, doc_count, 256),
+        grid=(pairs,),
+        in_specs=[
+            pl.BlockSpec((total, 384), lambda j: (0, j)),
+            pl.BlockSpec((total, 128), lambda j: (0, j)),
+            pl.BlockSpec((1, 8, total), lambda j: (j, 0, 0)),
+            pl.BlockSpec((2, 128, span - 128), lambda j: (j, 0, 0)),
+            pl.BlockSpec(mask.shape, lambda j: (0, 0, 0)),
+        ],
+        out_specs=[
+            pl.BlockSpec((total, 384), lambda j: (0, j)),
+            pl.BlockSpec((1, 8, span), lambda j: (j, 0, 0)),
+        ],
+        out_shape=[
+            jax.ShapeDtypeStruct((total, width), BF),
+            jax.ShapeDtypeStruct((pairs, 8, span), F32),
+        ],
+        scratch_shapes=[pltpu.VMEM((2, 128, span), F32)],
+        compiler_params=pltpu.CompilerParams(vmem_limit_bytes=40 << 20),
+        name="attend_back",
+    )(qkv, d_ctx, lse, table, mask)
+
+def query_mask(lengths, slots):
+    per = 128 // slots
+    live = (jnp.arange(slots, dtype=jnp.int32)[None, :] < lengths[:, None]).reshape(-1, 128)
+    owner = jnp.arange(128, dtype=jnp.int32) // slots
+    same = owner[:, None] == owner[None, :]
+    return (live[:, :, None] & same[None]).astype(F32)
+
+def pair_columns(w):
+    q, k, v = w
+    rows, width = q.shape
+    pack = jnp.stack([x.reshape(rows, width // 128, 128) for x in (q, k, v)], axis=2)
+    return pack.reshape(rows, 3 * width)
+
+
+def score_kernel(peers, doc_len, slots, emb_ref, picks_ref, live_ref, goal_ref, loss_ref, d_emb_ref,
+                 q_own, q_all, p_all, weighed, totals, pool_out, pool_in, grad_out, grad_in, dq_out, dq_in, docs_t, d_docs,
+                 s_q, r_q, s_p, r_p, s_pool, r_pool, s_grad, r_grad, s_dq, r_dq):
+    dp = lax.axis_index("dp"); me = lax.axis_index("wide")
+    tokens = q_own.shape[0]
+    feat = emb_ref.shape[1]
+    half = tokens // 2
+    scale = feat ** -0.5
+    barrier = pltpu.get_barrier_semaphore()
+    def other(k):
+        return lax.rem(me + k, peers)
+    def each(fn):
+        @pl.loop(1, peers)
+        def _(k):
+            fn(other(k))
+    each(lambda o: pl.semaphore_signal(barrier, inc=1, device_id=(dp, o), device_id_type=MESH))
+    q_own[...] = emb_ref[2 * doc_len :, :]
+    q_all[me] = q_own[...]
+    p_all[me] = picks_ref[...]
+    pl.semaphore_wait(barrier, peers - 1)
+    def send(src, dst, ss, rs, o):
+        return pltpu.make_async_remote_copy(src_ref=src, dst_ref=dst, send_sem=ss, recv_sem=rs, device_id=(dp, o), device_id_type=MESH)
+    def picks_to(o): return send(picks_ref, p_all.at[me], s_p.at[o], r_p.at[me], o)
+    def picks_from(o): return send(picks_ref, p_all.at[o], s_p.at[o], r_p.at[o], o)
+    def q_to(o): return send(q_own, q_all.at[me], s_q.at[o], r_q.at[me], o)
+    def q_from(o): return send(q_own, q_all.at[o], s_q.at[o], r_q.at[o], o)
+    def pool_to(o): return send(pool_out.at[o], pool_in.at[me], s_pool.at[o], r_pool.at[me], o)
+    def pool_from(o): return send(pool_out.at[o], pool_in.at[o], s_pool.at[o], r_pool.at[o], o)
+    def grad_to(o): return send(grad_out.at[o], grad_in.at[me], s_grad.at[o], r_grad.at[me], o)
+    def grad_from(o): return send(grad_out.at[o], grad_in.at[o], s_grad.at[o], r_grad.at[o], o)
+    def dq_to(o): return send(dq_out.at[o], dq_in.at[me], s_dq.at[o], r_dq.at[me], o)
+    def dq_from(o): return send(dq_out.at[o], dq_in.at[o], s_dq.at[o], r_dq.at[o], o)
+    def started(o):
+        picks_to(o).start(); q_to(o).start()
+    each(started)
+    docs2 = jnp.concatenate([emb_ref[0:doc_len, :], emb_ref[doc_len : 2 * doc_len, :]], axis=1)
+    docs_t[...] = docs2.astype(F32).T.astype(BF)
+    row = lax.broadcasted_iota(jnp.int32, (tokens, 1), 0)
+    lane = lax.broadcasted_iota(jnp.int32, (1, tokens), 1)
+    def two_docs(o):
+        q = q_all[o]
+        none = jnp.zeros_like(q)
+        return jnp.concatenate([jnp.where(row < half, q, none), jnp.where(row < half, none, q)], axis=1)
+    chunk = 64
+    base = me * doc_len
+    def forward(o):
+        picks = p_all[o] - base
+        found = jnp.zeros((1, tokens), F32)
+        weight = jnp.zeros((1, tokens), F32)
+        s = lax.dot_general(docs2, two_docs(o), (((1,), (1,)), ((), ())), preferred_element_type=F32) * scale
+        e = jnp.exp(s)
+        for at in range(0, doc_len, chunk):
+            place = lax.broadcasted_iota(jnp.int32, (chunk, tokens), 0) + at
+            count = jnp.zeros((chunk, tokens), jnp.int32)
+            for k in range(picks.shape[0]):
+                count = count + (picks[k : k + 1, :] == place).astype(jnp.int32)
+            multiple = count.astype(F32)
+            w = multiple * e[at : at + chunk]
+            weighed[o, at : at + chunk, :] = w
+            found = found + jnp.sum(multiple, axis=0, keepdims=True)
+            weight = weight + jnp.sum(w, axis=0, keepdims=True)
+        weight = weight + (found == 0).astype(F32)
+        totals[o] = jnp.broadcast_to(weight, (8, tokens))
+        pool_out[o] = jnp.broadcast_to(jnp.log(weight), (8, tokens))
+    def forward_peer(o):
+        picks_from(o).wait_recv(); q_from(o).wait_recv()
+        forward(o)
+        pool_to(o).start()
+    forward(me)
+    pool_in[me] = pool_out[me]
+    each(forward_peer)
+    each(lambda o: pool_from(o).wait_recv())
+    pooled = pool_in[:, 0, :]
+    mine = picks_ref[...]
+    hits = []
+    for w in range(peers):
+        inside = ((mine >= w * doc_len) & (mine < (w + 1) * doc_len)).astype(F32)
+        hits.append(jnp.max(inside, axis=0, keepdims=True))
+    hit = jnp.concatenate(hits, axis=0)
+    live = live_ref[0:1, :]
+    own_row = lax.broadcasted_iota(jnp.int32, (tokens, tokens), 0) // slots
+    own_col = lax.broadcasted_iota(jnp.int32, (tokens, tokens), 1) // slots
+    same = (own_row == own_col).astype(F32)
+    def per_query(v):
+        return jnp.dot(v, same, precision=lax.Precision.HIGHEST, preferred_element_type=F32)
+    divisor = jnp.maximum(per_query(hit * live), 1.0)
+    logits = score_scale * per_query(pooled * live) / divisor
+    top = jnp.max(logits, axis=0, keepdims=True)
+    shifted = jnp.exp(logits - top)
+    total = jnp.sum(shifted, axis=0, keepdims=True)
+    doc_id = lax.broadcasted_iota(jnp.int32, (peers, tokens), 0)
+    chosen = (doc_id == goal_ref[0:1, :]).astype(F32)
+    loss = top + jnp.log(total) - jnp.sum(chosen * logits, axis=0, keepdims=True)
+    loss_ref[...] = jnp.broadcast_to(loss, loss_ref.shape)
+    d_pooled = score_scale * (shifted / total - chosen) / divisor * live
+    for w in range(peers):
+        grad_out[w] = jnp.broadcast_to(d_pooled[w : w + 1], (8, tokens))
+    each(lambda o: grad_to(o).start())
+    grad_in[me] = grad_out[me]
+    d_docs[...] = jnp.zeros_like(d_docs)
+    def backward(o):
+        factor = grad_in[o][0:1] / totals[o][0:1] * scale
+        d_raw = (weighed[o] * factor).astype(BF)
+        d_docs[...] += jnp.dot(d_raw, two_docs(o), preferred_element_type=F32)
+        both = jnp.dot(docs_t[...], d_raw, preferred_element_type=F32)
+        d_q = jnp.where(lane < half, both[0:feat], both[feat : 2 * feat])
+        dq_out[o] = d_q.T.astype(BF)
+    def backward_peer(o):
+        grad_from(o).wait_recv()
+        backward(o)
+        dq_to(o).start()
+    each(backward_peer)
+    backward(me)
+    d_emb_ref[0:doc_len, :] = d_docs[:, 0:feat].astype(BF)
+    d_emb_ref[doc_len : 2 * doc_len, :] = d_docs[:, feat : 2 * feat].astype(BF)
+    dq_in[me] = dq_out[me]
+    each(lambda o: dq_from(o).wait_recv())
+    total_q = dq_in[0].astype(F32)
+    for w in range(1, peers):
+        total_q = total_q + dq_in[w].astype(F32)
+    d_emb_ref[2 * doc_len :, :] = total_q.astype(BF)
+    def sent(o):
+        picks_to(o).wait_send(); q_to(o).wait_send(); pool_to(o).wait_send(); grad_to(o).wait_send(); dq_to(o).wait_send()
+    each(sent)
+
+def score(emb, picks, live, goal, doc_len, slots, peers):
+    tokens = picks.shape[1]
+    feat = emb.shape[1]
+    V = pltpu.VMEM
+    dma = pltpu.SemaphoreType.DMA
+    return pl.pallas_call(
+        functools.partial(score_kernel, peers, doc_len, slots),
+        out_shape=[jax.ShapeDtypeStruct((8, tokens), F32), jax.ShapeDtypeStruct(emb.shape, BF)],
+        in_specs=[pl.BlockSpec(memory_space=pltpu.VMEM)] * 4,
+        out_specs=[pl.BlockSpec(memory_space=pltpu.VMEM)] * 2,
+        scratch_shapes=[
+            V((tokens, feat), BF), V((peers, tokens, feat), BF), V((peers,) + picks.shape, jnp.int32),
+            V((peers, doc_len, tokens), F32), V((peers, 8, tokens), F32),
+            V((peers, 8, tokens), F32), V((peers, 8, tokens), F32), V((peers, 8, tokens), F32), V((peers, 8, tokens), F32),
+            V((peers, tokens, feat), BF), V((peers, tokens, feat), BF), V((2 * feat, doc_len), BF), V((doc_len, 2 * feat), F32),
+        ] + [dma((peers,))] * 10,
+        compiler_params=pltpu.CompilerParams(collective_id=2, has_side_effects=True, vmem_limit_bytes=48 << 20),
+        name="score",
+    )(emb, picks, live, goal)
 
 
 def contract_rows(left_mat, right_mat):
@@ -513,294 +757,34 @@
     return (inverse * scaled - values * inverse * inverse * inverse * inner_mean, gain_grad)
 
 
-def bucket_onehot(length, bucket_count):
-    places = jnp.arange(length, dtype=jnp.int32)
-    offset_ij = places[None, :] - places[:, None]
-    distance = jnp.abs(offset_ij)
-    steps_far = jnp.zeros_like(distance)
-    for power_step in range(1, 8):
-        steps_far = steps_far + (distance * distance >= 64 * 2**power_step).astype(jnp.int32)
-    bucket_ids = jnp.where(offset_ij > 0, 16, 0) + jnp.where(distance < 8, distance, 8 + steps_far)
+def two_level(shards):
     return (
-        bucket_ids[:, :, None] == jnp.arange(bucket_count, dtype=jnp.int32)[None, None, :]
-    ).astype(jnp.float32)
-
-
-def attention_scores(queries_h, keys_h, bias_full, valid_keys):
-    scores = (
-        jnp.einsum("bqhd,bkhd->bhqk", queries_h, keys_h, preferred_element_type=jnp.float32)
-        + bias_full[None]
+        lax.axis_size("dp") == 4
+        and lax.axis_size("wide") % 4 == 0
+        and all(s.shape[0] % 8 == 0 for s in shards)
     )
-    return jnp.where(valid_keys[:, None, None, :], scores, mask_fill)
-
-
-def encode_forward(tokens, valid_keys, bias_full, full_weights):
-    (
-        w_query,
-        w_key,
-        w_value,
-        w_out,
-        w_gate,
-        w_up,
-        w_down,
-        w_proj,
-        gain_attn,
-        gain_ffn,
-        gain_final,
-    ) = full_weights
-    batch_size, length, width_size = tokens.shape
-    head_count = bias_full.shape[0]
-    flat_rows = tokens.astype(jnp.float32).reshape(batch_size * length, width_size)
-    normed_full, inverse_one = rms_forward(flat_rows, gain_attn.astype(jnp.float32))
-    normed = normed_full.astype(jnp.bfloat16)
-
-    def split_heads(weight):
-        return (
-            matmul(normed, weight).astype(jnp.bfloat16).reshape(batch_size, length, head_count, -1)
-        )
-
-    queries_h = split_heads(w_query)
-    keys_h = split_heads(w_key)
-    values_h = split_heads(w_value)
-    scores = attention_scores(queries_h, keys_h, bias_full, valid_keys)
-    row_top = jnp.max(scores, axis=-1, keepdims=True)
-    shifted = jnp.exp(scores - row_top)
-    row_totals = jnp.sum(shifted, axis=-1, keepdims=True)
-    probs_attn = shifted / row_totals
-    log_total = row_top + jnp.log(row_totals)
-    context = jnp.einsum(
-        "bhqk,bkhd->bqhd",
-        probs_attn.astype(jnp.bfloat16),
-        values_h,
-        preferred_element_type=jnp.float32,
-    )
-    context = context.astype(jnp.bfloat16).reshape(batch_size * length, width_size)
-    hidden = flat_rows + matmul(context, w_out)
-    normed_two_full, inverse_two = rms_forward(hidden, gain_ffn.astype(jnp.float32))
-    normed_two = normed_two_full.astype(jnp.bfloat16)
-    gate_pre = matmul(normed_two, w_gate)
-    up_pre = matmul(normed_two, w_up)
-    activated = (jax.nn.gelu(gate_pre) * up_pre).astype(jnp.bfloat16)
-    layer_out = hidden + matmul(activated, w_down)
-    normed_end_full, inverse_end = rms_forward(layer_out, gain_final.astype(jnp.float32))
-    normed_end = normed_end_full.astype(jnp.bfloat16)
-    embedded = matmul(normed_end, w_proj).astype(jnp.bfloat16)
-    kept_state = (
-        flat_rows,
-        inverse_one,
-        normed,
-        queries_h,
-        keys_h,
-        values_h,
-        log_total,
-        context,
-        hidden,
-        inverse_two,
-        normed_two,
-        gate_pre,
-        up_pre,
-        activated,
-        layer_out,
-        inverse_end,
-        normed_end,
-    )
-    return (embedded, kept_state)
-
-
-def encode_backward(grad_emb, kept_state, valid_keys, bias_full, onehot_table, full_weights):
-    (
-        w_query,
-        w_key,
-        w_value,
-        w_out,
-        w_gate,
-        w_up,
-        w_down,
-        w_proj,
-        gain_attn,
-        gain_ffn,
-        gain_final,
-    ) = full_weights
-    (
-        flat_rows,
-        inverse_one,
-        normed,
-        queries_h,
-        keys_h,
-        values_h,
-        log_total,
-        context,
-        hidden,
-        inverse_two,
-        normed_two,
-        gate_pre,
-        up_pre,
-        activated,
-        layer_out,
-        inverse_end,
-        normed_end,
-    ) = kept_state
-    row_count, width_size = flat_rows.shape
-    grad_low = grad_emb.astype(jnp.bfloat16)
-    proj_grad = contract_rows(normed_end, grad_low)
-    d_normed_end = contract_cols(grad_low, w_proj)
-    d_layer, final_gain_grad = rms_backward(
-        layer_out, inverse_end, gain_final.astype(jnp.float32), d_normed_end
-    )
-    d_layer_low = d_layer.astype(jnp.bfloat16)
-    down_grad = contract_rows(activated, d_layer_low)
-    d_activated = contract_cols(d_layer_low, w_down)
-    unused_value, pull_back = jax.vjp(
-        lambda first_arg, second_arg: jax.nn.gelu(first_arg) * second_arg, gate_pre, up_pre
-    )
-    d_gate, d_up = pull_back(d_activated)
-    d_gate = d_gate.astype(jnp.bfloat16)
-    d_up = d_up.astype(jnp.bfloat16)
-    gate_grad = contract_rows(normed_two, d_gate)
-    up_grad = contract_rows(normed_two, d_up)
-    d_normed_two = contract_cols(d_gate, w_gate) + contract_cols(d_up, w_up)
-    d_hidden_norm, ffn_gain_grad = rms_backward(
-        hidden, inverse_two, gain_ffn.astype(jnp.float32), d_normed_two
-    )
-    d_hidden = d_layer + d_hidden_norm
-    d_hidden_low = d_hidden.astype(jnp.bfloat16)
-    out_grad = contract_rows(context, d_hidden_low)
-    d_context = contract_cols(d_hidden_low, w_out).astype(jnp.bfloat16).reshape(queries_h.shape)
-    scores = attention_scores(queries_h, keys_h, bias_full, valid_keys)
-    probs_attn = jnp.exp(scores - log_total)
-    d_probs = jnp.einsum("bqhd,bkhd->bhqk", d_context, values_h, preferred_element_type=jnp.float32)
-    d_values = jnp.einsum(
-        "bhqk,bqhd->bkhd",
-        probs_attn.astype(jnp.bfloat16),
-        d_context,
-        preferred_element_type=jnp.float32,
-    )
-    d_values = d_values.astype(jnp.bfloat16).reshape(row_count, width_size)
-    d_scores = probs_attn * (d_probs - jnp.sum(probs_attn * d_probs, axis=-1, keepdims=True))
-    table_grad = jnp.einsum(
-        "hij,ijb->bh", jnp.sum(d_scores, axis=0), onehot_table, precision=top_precision
-    )
-    d_scores_low = d_scores.astype(jnp.bfloat16)
-    d_queries = jnp.einsum(
-        "bhqk,bkhd->bqhd", d_scores_low, keys_h, preferred_element_type=jnp.float32
-    )
-    d_queries = d_queries.astype(jnp.bfloat16).reshape(row_count, width_size)
-    d_keys = jnp.einsum(
-        "bhqk,bqhd->bkhd", d_scores_low, queries_h, preferred_element_type=jnp.float32
-    )
-    d_keys = d_keys.astype(jnp.bfloat16).reshape(row_count, width_size)
-    query_w_grad = contract_rows(normed, d_queries)
-    key_w_grad = contract_rows(normed, d_keys)
-    value_w_grad = contract_rows(normed, d_values)
-    d_normed = (
-        contract_cols(d_queries, w_query)
-        + contract_cols(d_keys, w_key)
-        + contract_cols(d_values, w_value)
-    )
-    d_flat, attn_gain_grad = rms_backward(
-        flat_rows, inverse_one, gain_attn.astype(jnp.float32), d_normed
-    )
-    grad_list = (
-        query_w_grad,
-        key_w_grad,
-        value_w_grad,
-        out_grad,
-        gate_grad,
-        up_grad,
-        down_grad,
-        proj_grad,
-        attn_gain_grad,
-        ffn_gain_grad,
-        final_gain_grad,
-    )
-    return (d_hidden + d_flat, grad_list, table_grad)
-
-
-def pool_rows(row_block, picks_block, doc_emb, positions):
-    scores_raw = contract_cols(row_block, doc_emb) * doc_emb.shape[1] ** (-0.5)
-    multiple = jnp.sum(
-        (picks_block[:, :, None] == positions[None, None, :]).astype(jnp.float32), axis=1
-    )
-    present = jnp.sum(multiple, axis=-1)
-    totals_sum = jnp.sum(multiple * jnp.exp(scores_raw), axis=-1) + (present == 0).astype(
-        jnp.float32
-    )
-    return (scores_raw, multiple, totals_sum)
-
-
-def score_forward(query_all, picks_all, doc_emb, positions):
-    row_count = query_all.shape[0]
-    block_size = min(block_rows, row_count)
-    block_count = row_count // block_size
-
-    def one_block(bundle):
-        scores_raw, multiple, totals_sum = pool_rows(bundle[0], bundle[1], doc_emb, positions)
-        return jnp.log(totals_sum)
-
-    pooled = lax.map(
-        one_block,
-        (
-            query_all.reshape(block_count, block_size, -1),
-            picks_all.reshape(block_count, block_size, -1),
-        ),
-    )
-    return pooled.reshape(row_count)
-
-
-def score_backward(query_all, picks_all, doc_emb, positions, pooled_grad):
-    row_count = query_all.shape[0]
-    block_size = min(block_rows, row_count)
-    block_count = row_count // block_size
-    scale_factor = doc_emb.shape[1] ** (-0.5)
-
-    def one_block(doc_acc, bundle):
-        row_block, picks_block, grad_block = bundle
-        scores_raw, multiple, totals_sum = pool_rows(row_block, picks_block, doc_emb, positions)
-        d_raw = (grad_block / totals_sum)[:, None] * multiple * jnp.exp(scores_raw) * scale_factor
-        d_low = d_raw.astype(jnp.bfloat16)
-        return (doc_acc + contract_rows(d_low, row_block), matmul(d_low, doc_emb))
-
-    start_acc = jnp.zeros(doc_emb.shape, jnp.float32)
-    doc_grad, query_blocks = lax.scan(
-        one_block,
-        start_acc,
-        (
-            query_all.reshape(block_count, block_size, -1),
-            picks_all.reshape(block_count, block_size, -1),
-            pooled_grad.reshape(block_count, block_size),
-        ),
-    )
-    return (doc_grad, query_blocks.reshape(row_count, -1))
-
-
-def query_loss(pooled_query, own_picks, lengths, goal_ids, doc_len):
-    wide_count, token_count = pooled_query.shape
-    query_count = lengths.shape[0]
-    slot_count = token_count // query_count
-    owner_doc = own_picks // doc_len
-    doc_ids = jnp.arange(wide_count, dtype=jnp.int32)
-    hit_mask = jnp.any(owner_doc[None, :, :] == doc_ids[:, None, None], axis=-1).astype(jnp.float32)
-    valid_mask = (
-        (jnp.arange(slot_count, dtype=jnp.int32)[None, :] < lengths[:, None])
-        .astype(jnp.float32)
-        .reshape(token_count)
-    )
-    counts = jnp.sum((hit_mask * valid_mask).reshape(wide_count, query_count, slot_count), axis=-1)
-    divisor = jnp.maximum(counts, 1.0)
-    summed = jnp.sum(
-        (pooled_query * valid_mask).reshape(wide_count, query_count, slot_count), axis=-1
-    )
-    logits = score_scale * summed / divisor
-    col_top = jnp.max(logits, axis=0, keepdims=True)
-    shifted = jnp.exp(logits - col_top)
-    col_totals = jnp.sum(shifted, axis=0, keepdims=True)
-    chosen = (doc_ids[:, None] == goal_ids[None, :]).astype(jnp.float32)
-    losses = col_top[0] + jnp.log(col_totals[0]) - jnp.sum(chosen * logits, axis=0)
-    d_logits = shifted / col_totals - chosen
-    d_pooled = (score_scale * d_logits / divisor)[:, :, None] * valid_mask.reshape(
-        1, query_count, slot_count
-    )
-    return (losses, d_pooled.reshape(wide_count, token_count))
+
+
+def gathered(shards):
+    if not two_level(shards):
+        return [lax.all_gather(s, ("dp", "wide"), axis=0, tiled=True) for s in shards]
+    zc = lax.axis_size("wide") // 2
+    padded = [(jnp.pad(s, ((0, -s.shape[0] % 16), (0, 0))), s.shape[0]) for s in shards]
+    return gather(padded, zc, 8 * zc)
+
+
+def scattered(grads, table):
+    n_dev = lax.axis_size("dp") * lax.axis_size("wide")
+    if not two_level([g[: g.shape[0] // n_dev] for g in grads]):
+        shards = [
+            lax.psum_scatter(g.astype(F32), ("dp", "wide"), scatter_dimension=0, tiled=True)
+            for g in grads
+        ]
+        return [*shards, lax.psum(table, ("dp", "wide"))]
+    flat = table.reshape(-1)
+    packed = jnp.pad(flat, (0, -flat.shape[0] % 1024)).reshape(-1, 128)
+    *shards, packed = reduce_scatter(grads, packed, lax.axis_size("wide") // 2)
+    return [*shards, packed.reshape(-1)[: flat.shape[0]].reshape(table.shape)]
 
 
 def local(
@@ -823,67 +807,95 @@
     rel_bias,
 ):
     micro_count, _, doc_len, width = doc_tokens.shape
-    query_count, slot_count = query_tokens.shape[1:3]
-    picks_width = retrieved.shape[3]
+    slots = query_tokens.shape[2]
+    doc_rows = micro_count * doc_len
     wide_count = lax.axis_size("wide")
-    bias_table = rel_bias.astype(jnp.float32)
-    onehot_doc = bucket_onehot(doc_len, rel_bias.shape[0])
-    onehot_query = bucket_onehot(slot_count, rel_bias.shape[0])
-    bias_doc = jnp.einsum("ijb,bh->hij", onehot_doc, bias_table, precision=top_precision)
-    bias_query = jnp.einsum("ijb,bh->hij", onehot_query, bias_table, precision=top_precision)
-    doc_valid = jnp.ones((1, doc_len), dtype=bool)
-    slot_ids = jnp.arange(slot_count, dtype=jnp.int32)
-    positions = lax.axis_index("wide") * doc_len + jnp.arange(doc_len, dtype=jnp.int32)
-    full_weights = gathered(q_weight, k_weight, v_weight, o_weight, gate_weight, up_weight, down_weight, proj_weight, attn_gain, ffn_gain, final_gain)
-    picks_group = lax.all_gather(retrieved, "wide", axis=1, tiled=True)
-    docs = doc_tokens.reshape(micro_count, doc_len, width)
-    queries = query_tokens.reshape(micro_count * query_count, slot_count, width)
-    query_valid = slot_ids[None, :] < query_lengths.reshape(-1)[:, None]
-    doc_emb, doc_state = encode_forward(docs, doc_valid, bias_doc, full_weights)
-    query_emb, query_state = encode_forward(queries, query_valid, bias_query, full_weights)
-    doc_emb = doc_emb.reshape(micro_count, doc_len, -1)
-    query_emb = query_emb.reshape(micro_count, query_count * slot_count, -1)
-    query_all = lax.all_gather(query_emb, "wide", axis=1, tiled=True)
-    pooled = jnp.stack([
-        score_forward(query_all[m], picks_group[m].reshape(-1, picks_width), doc_emb[m], positions)
-        for m in range(micro_count)
-    ])
-    pooled_query = lax.all_to_all(
-        pooled.reshape(micro_count, wide_count, -1), "wide", split_axis=1, concat_axis=1, tiled=True
+    p_size = proj_weight.shape[1]
+    bucket_count, head_count = rel_bias.shape
+    pairs = width // 128
+    gains = jnp.stack([attn_gain, ffn_gain, final_gain], axis=1)
+    last = jnp.concatenate([proj_weight, jnp.pad(gains, ((0, 0), (0, 128 - gains.shape[1])))], axis=1)
+    w_qkv, w_out, w_last, w_gate, w_up, w_down = gathered(
+        [pair_columns((q_weight, k_weight, v_weight)), o_weight, last, gate_weight, up_weight, down_weight]
     )
-    results = [
-        query_loss(pooled_query[m], retrieved[m].reshape(-1, picks_width), query_lengths[m], targets[m], doc_len)
-        for m in range(micro_count)
-    ]
-    losses_out = jnp.stack([r[0] for r in results])
-    d_pooled = jnp.stack([r[1] for r in results])
-    d_pooled_doc = lax.all_to_all(d_pooled, "wide", split_axis=1, concat_axis=1, tiled=True)
-    backs = [
-        score_backward(
-            query_all[m],
-            picks_group[m].reshape(-1, picks_width),
-            doc_emb[m],
-            positions,
-            d_pooled_doc[m].reshape(-1),
-        )
-        for m in range(micro_count)
-    ]
-    doc_emb_grad = jnp.concatenate([b[0] for b in backs])
-    query_all_grad = jnp.stack([b[1] for b in backs])
-    query_emb_grad = sent_and_summed(query_all_grad.astype(jnp.bfloat16), "wide", 1)
-    doc_in_grad, doc_grads, doc_table = encode_backward(
-        doc_emb_grad, doc_state, doc_valid, bias_doc, onehot_doc, full_weights
+    w_proj = w_last[:, :p_size]
+    gain_attn, gain_ffn, gain_final = (w_last[:, p_size + i].astype(F32) for i in range(3))
+    hot = diagonal_onehot(doc_len, bucket_count)
+    diag = jnp.dot(rel_bias.astype(F32).T, hot.T, precision=top_precision)
+    diag = jnp.pad(diag.reshape(pairs, 2, -1), ((0, 0), (0, 6), (0, 0)))
+    mask = query_mask(query_lengths.reshape(-1), slots)
+    rows = jnp.concatenate(
+        [doc_tokens.reshape(doc_rows, width), query_tokens.reshape(-1, width)], axis=0
+    ).astype(F32)
+    normed_full, inverse_one = rms_forward(rows, gain_attn)
+    normed = normed_full.astype(BF)
+    qkv = matmul(normed, w_qkv).astype(BF)
+    context, lse, table = attend(qkv, diag, mask, doc_len, micro_count)
+    hidden = rows + matmul(context, w_out)
+    normed_two_full, inverse_two = rms_forward(hidden, gain_ffn)
+    normed_two = normed_two_full.astype(BF)
+    gate_pre = matmul(normed_two, w_gate)
+    up_pre = matmul(normed_two, w_up)
+    activated = (jax.nn.gelu(gate_pre) * up_pre).astype(BF)
+    layer_out = hidden + matmul(activated, w_down)
+    normed_end_full, inverse_end = rms_forward(layer_out, gain_final)
+    normed_end = normed_end_full.astype(BF)
+    embedded = matmul(normed_end, w_proj).astype(BF)
+    picks = retrieved.reshape(-1, retrieved.shape[3]).T
+    tokens = picks.shape[1]
+    live = (jnp.arange(slots, dtype=jnp.int32)[None, :] < query_lengths.reshape(-1)[:, None]).astype(F32)
+    live = jnp.broadcast_to(live.reshape(1, tokens), (8, tokens))
+    goal = jnp.broadcast_to(jnp.repeat(targets.reshape(-1), slots)[None, :], (8, tokens))
+    loss_rows, d_embedded = score(embedded, picks, live, goal, doc_len, slots, wide_count)
+    losses_out = loss_rows[0].reshape(-1, slots)[:, 0].reshape(targets.shape)
+    proj_grad = contract_rows(normed_end, d_embedded)
+    d_normed_end = contract_cols(d_embedded, w_proj)
+    d_layer, final_gain_grad = rms_backward(layer_out, inverse_end, gain_final, d_normed_end)
+    d_layer_low = d_layer.astype(BF)
+    down_grad = contract_rows(activated, d_layer_low).astype(BF)
+    d_activated = contract_cols(d_layer_low, w_down)
+    _, pull_back = jax.vjp(
+        lambda first_arg, second_arg: jax.nn.gelu(first_arg) * second_arg, gate_pre, up_pre
     )
-    query_in_grad, query_grads, query_table = encode_backward(
-        query_emb_grad.reshape(-1, query_emb_grad.shape[-1]), query_state, query_valid, bias_query, onehot_query, full_weights
+    d_gate, d_up = pull_back(d_activated)
+    d_gate = d_gate.astype(BF)
+    d_up = d_up.astype(BF)
+    gate_grad = contract_rows(normed_two, d_gate).astype(BF)
+    up_grad = contract_rows(normed_two, d_up).astype(BF)
+    d_normed_two = contract_cols(d_gate, w_gate) + contract_cols(d_up, w_up)
+    d_hidden_norm, ffn_gain_grad = rms_backward(hidden, inverse_two, gain_ffn, d_normed_two)
+    d_hidden = d_layer + d_hidden_norm
+    d_hidden_low = d_hidden.astype(BF)
+    out_grad = contract_rows(context, d_hidden_low).astype(BF)
+    d_context = contract_cols(d_hidden_low, w_out).astype(BF)
+    d_qkv, d_diag = attend_back(qkv, d_context, lse, table, mask, doc_len, micro_count)
+    table_grad = jnp.dot(hot.T, d_diag[:, :2].reshape(head_count, -1).T, precision=top_precision)
+    qkv_grad = contract_rows(normed, d_qkv).astype(BF)
+    d_normed = contract_cols(d_qkv, w_qkv)
+    d_rows, attn_gain_grad = rms_backward(rows, inverse_one, gain_attn, d_normed)
+    d_rows = d_hidden + d_rows
+    gain_grads = jnp.stack([attn_gain_grad, ffn_gain_grad, final_gain_grad], axis=1)
+    last_grad = jnp.concatenate([proj_grad, jnp.pad(gain_grads, ((0, 0), (0, 125)))], axis=1).astype(BF)
+    s_qkv, s_out, s_last, s_gate, s_up, s_down, s_table = scattered(
+        [qkv_grad, out_grad, last_grad, gate_grad, up_grad, down_grad], table_grad
     )
-    grads = jax.tree.map(jnp.add, doc_grads, query_grads)
-    shards = scattered(grads, doc_table + query_table)
+    apart = s_qkv.reshape(-1, pairs, 3, 128)
     return (
         losses_out,
-        doc_in_grad.reshape(doc_tokens.shape),
-        query_in_grad.reshape(query_tokens.shape),
-        *shards,
+        d_rows[:doc_rows].reshape(doc_tokens.shape),
+        d_rows[doc_rows:].reshape(query_tokens.shape),
+        apart[:, :, 0].reshape(-1, width),
+        apart[:, :, 1].reshape(-1, width),
+        apart[:, :, 2].reshape(-1, width),
+        s_out,
+        s_gate,
+        s_up,
+        s_down,
+        s_last[:, :p_size],
+        s_last[:, p_size],
+        s_last[:, p_size + 1],
+        s_last[:, p_size + 2],
+        s_table,
     )
 
 

time: 782 us -> 455 us (0.58)
  matrix products: 281 us -> 96.7 us
  Pallas kernels: 189 us -> 309 us
  other arithmetic: 117 us -> 10.8 us
  local copies, waits for them, and re-layouts: 133 us -> 31 us
  blocking collectives: 30.6 us -> 0 us
  starting transfers between devices: 14.1 us -> 0 us
    dot_general x16 -> x2, matrix products: 121 us -> 1.72 us  [the longest x1 1 us: local(): diag = jnp.dot(rel_bias.astype(F32).T, hot.T, precision=top_precision)]
    pallas_call x0 -> x3, Pallas kernels: none -> 88.8 us  [the longest x1 31.6 us: score(): pl.pallas_call(functools.partial(score_kernel, peers, doc_len, slots), ou...]
    reduce_sum x10 -> x0, other arithmetic: 70.7 us -> none  [the longest x2 33.3 us: encode_backward(): jnp.sum(d_scores, axis=0)]
    dot_general x18 -> x6, matrix products: 70.3 us -> 32.4 us  [contract_cols(): lax.dot_general(left_mat, right_mat, (((1,), (1,)), ((), ())), preferred_...]
    all_gather x2 -> x0, blocking collectives: 30.6 us -> none  [the longest x1 15.7 us: local(): query_all = lax.all_gather(query_emb, 'wide', axis=1, tiled=True)]
    reduce_sum x4 -> x0, local copies, waits for them, and re-layouts: 25.4 us -> none  [the longest x2 20.2 us: encode_backward(): jnp.sum(d_scores, axis=0)]
    reshape x14 -> x8, local copies, waits for them, and re-layouts: 25.4 us -> 2.04 us  [the longest x1 0.9 us: local(): picks = retrieved.reshape(-1, retrieved.shape[3]).T]
    convert_element_type x12 -> x0, local copies, waits for them, and re-layouts: 21.4 us -> none  [the longest x3 7.81 us: split_heads(): matmul(normed, weight).astype(jnp.bfloat16)]
  transfers between devices with their start and end apart: 3 -> 0, of which waited for: 1 -> 0; matrix products, arithmetic and copies ran while one was open for 10% -> 0% of each run, Pallas kernels for 0% -> 0%
where the time goes in v2:
time: 455 us; the launch traced here: 450 us
  Pallas kernels  309 us (68%)
  matrix products  96.7 us (21%)
  local copies, waits for them, and re-layouts  31 us (7%)
  other arithmetic  10.8 us (2%)
    pallas_call x1, Pallas kernels, reduce_scatter(): pl.pallas_call(functools.partial(reduce_kernel, zc, count), out_shape=out...  123 us
    pallas_call x1, Pallas kernels, gather(): pl.pallas_call(functools.partial(gather_kernel, zc, count), out_shape=out...  97.5 us
    dot_general x6, matrix products, contract_rows(): lax.dot_general(left_mat, right_mat, (((0,), (0,)), ((), ())), preferred_...  33.9 us
    dot_general x6, matrix products, contract_cols(): lax.dot_general(left_mat, right_mat, (((1,), (1,)), ((), ())), preferred_...  32.4 us
    pallas_call x1, Pallas kernels, score(): pl.pallas_call(functools.partial(score_kernel, peers, doc_len, slots), ou...  31.6 us
    pallas_call x1, Pallas kernels, attend_back(): pl.pallas_call(functools.partial(attend_back_kernel, doc_len, doc_count,...  30.3 us
    dot_general x6, matrix products, matmul(): return jnp.dot(left_mat, right_mat, preferred_element_type=jnp.float32)  28.7 us
    pallas_call x1, Pallas kernels, attend(): pl.pallas_call(functools.partial(attend_kernel, doc_len, doc_count, 256),...  26.9 us

profile of v2, /device:TPU:1, one launch (start us, length us, event | category | flops | bytes accessed | tf_op | source)
XLA Modules:
  0.0 449.6 jit_solution(6843119785684226821)
XLA Ops:
  4.3 1.9 fusion.14
  11.9 97.5 %gather_weights.1 = (bf16[768,2304]{1,0:T(8,128)(2,1)S(1)}, bf16[768,768]{1,0:T(8,128)(2,1)S(1)}, bf16[768,256]{1,0:T(8,128)(2,1)S(1)}, bf16[768,2048]{1,0:T(8,1...) custom-call(bf16[32,2304]{1,0:T(8,128)(2,1)S(1)} %pad.36.refs_0_, ...), custom_call_target="tpu_custom_call" | custom-call | tf_op jit(solution)/shard_map/gather_weights/pallas_call | solution.py:184
  112.9 5.3 %convolution_convert_fusion.qkv_ref = bf16[1152,2304]{1,0:T(8,128)(2,1)S(1)} fusion(bf16[768,2304]{1,0:T(8,128)(2,1)S(1)} %get-tuple-element.36, f32[768]{0:T(1024)S(1)} %get-tuple-element.108, f32[1152]{0:T(1024)S(1)} %add_rsqrt_fusion.2, bf16[128,768]{1,0:T(8,128)(2,1)S(1)} %bitcast.64, bf16[1024,768]{1,0:T(8,128)(2,1)S(1)} %bitcast.57), kind=kOutput, calls=%fused_computation.2 | convolution fusion | flops 4085710848 | bytes 10624512 | tf_op jit(solution)/shard_map/dot_general | solution.py:745
  118.3 26.9 %attend.1 = (bf16[1152,768]{1,0:T(8,128)(2,1)S(1)}, f32[6,8,1152]{2,1,0:T(8,128)S(1)}, f32[12,128,896]{2,1,0:T(8,128)S(1)}) custom-call(bf16[1152,2304]{1,0:T(8,128)(2,1)S(1)} %convolution_convert_fusion.qkv_ref, f32[6,8,1024]{2,1,0:T(8,128)S(1)} %pad.42.diag_ref, f32[1,128,128]{2,1,0:T(8,128)S(1)} %and_convert_fusion.mask_ref), custom_call_target="tpu_custom_call" | custom-call | tf_op jit(solution)/shard_map/attend/pallas_call | solution.py:473
  145.2 1.7 multiply_reduce_fusion.5
  149.9 6.3 %fusion.55 = f32[1152,2048]{1,0:T(8,128)} fusion(bf16[1152,768]{1,0:T(8,128)(2,1)S(1)} %multiply_convert_fusion.3, bf16[768,2048]{1,0:T(8,128)(2,1)S(1)} %get-tuple-element.39), kind=kOutput, calls=%fused_computation.119 | convolution fusion | flops 3623878656 | bytes 14352384 | tf_op jit(solution)/shard_map/dot_general | solution.py:745
  156.2 10.6 %multiply_convert_fusion.1 = (bf16[1152,2048]{1,0:T(8,128)(2,1)S(1)}, f32[1152,2048]{1,0:T(8,128)}) fusion(f32[1152,2048]{1,0:T(8,128)} %fusion.55, bf16[1152,768]{1,0:T(8,128)(2,1)S(1)} %multiply_convert_fusion.3, bf16[768,2048]{1,0:T(8,128)(2,1)S(1)} %get-tuple-element.40), kind=kOutput, calls=%fused_computation.11 | convolution fusion | flops 3647471616 | bytes 28508160 | tf_op jit(solution)/shard_map/dot_general | solution.py:745
  166.8 4.1 multiply_reduce_fusion.4
  171.6 31.6 %score.1 = (f32[8,128]{1,0:T(8,128)S(1)}, bf16[1152,128]{1,0:T(8,128)(2,1)S(1)}) custom-call(bf16[1152,128]{1,0:T(8,128)(2,1)S(1)} %convolution_convert_fusion.6.emb_ref, s32[32,128]{1,0:T(8,128)S(1)} %bitcast.55, f32[8,128]{1,0:T(8,128)S(1)} %broadcast_in_dim.15.live_ref, s32[8,128]{1,0:T(8,128)S(1)} %broadcast_in_dim.18.goal_ref), custom_call_target="tpu_custom_call" | custom-call | tf_op jit(solution)/shard_map/score/pallas_call | solution.py:716
  204.0 3.8 convolution_convert_fusion.8
  210.8 16.1 %multiply_convert_fusion = (bf16[1152,2048]{1,0:T(8,128)(2,1)}, bf16[1152,2048]{1,0:T(8,128)(2,1)}) fusion(f32[1152,2048]{1,0:T(8,128)} %fusion.55, f32[1152,2048]{1,0:T(8,128)} %get-tuple-element.120, bf16[2048,768]{1,0:T(8,128)(2,1)S(1)} %copy-done.20, f32[1152,768]{1,0:T(8,128)S(1)} %multiply_subtract_fusion), kind=kOutput, calls=%fused_computation.10 | convolution fusion | flops 3681386496 | bytes 34996224 | tf_op jit(solution)/shard_map/dot_general | solution.py:739
  227.0 8.6 %convolution_convert_fusion.2.refs_5_ = bf16[2048,768]{1,0:T(8,128)(2,1)} fusion(bf16[1152,2048]{1,0:T(8,128)(2,1)} %copy-done.41, f32[1152,768]{1,0:T(8,128)S(1)} %multiply_subtract_fusion), kind=kOutput, calls=%fused_computation.42 | convolution fusion | flops 3626336256 | bytes 11403264 | tf_op jit(solution)/shard_map/dot_general | solution.py:733
  235.6 3.9 fusion.56
  239.6 4.7 %multiply_reduce_fusion.1 = (bf16[768]{0:T(1024)(128)(2,1)S(1)}, f32[1152]{0:T(1024)S(1)}, f32[1152,768]{1,0:T(8,128)S(1)}) fusion(f32[1152,768]{1,0:T(8,128)S(1)} %copy-done.31, f32[1152]{0:T(1024)S(1)} %add_rsqrt_fusion.1, f32[768]{0:T(1024)S(1)} %get-tuple-element.107, f32[1152,768]{1,0:T(8,128)S(1)} %fusion.56, bf16[1152,2048]{1,0:T(8,128)(2,1)S(1)} %bitcast.79, ...), kind=kOutput, calls=%fused_computation.33 | convolution fusion | flops 3630069760 | bytes 18494976 | tf_op jit(solution)/shard_map/dot_general | solution.py:739
  244.3 5.7 %convolution_convert_fusion.3.refs_4_ = bf16[768,2048]{1,0:T(8,128)(2,1)} fusion(bf16[1152,768]{1,0:T(8,128)(2,1)S(1)} %multiply_convert_fusion.3, bf16[1152,2048]{1,0:T(8,128)(2,1)S(1)} %bitcast.79), kind=kOutput, calls=%fused_computation.43 | convolution fusion | flops 3625451520 | bytes 9633792 | tf_op jit(solution)/shard_map/dot_general | solution.py:733
  250.0 6.2 %convolution_convert_fusion.4.refs_3_ = bf16[768,2048]{1,0:T(8,128)(2,1)S(1)} fusion(bf16[1152,768]{1,0:T(8,128)(2,1)} %copy-done.34, bf16[1152,2048]{1,0:T(8,128)(2,1)S(1)} %copy-done.40), kind=kOutput, calls=%fused_computation.44 | convolution fusion | flops 3625451520 | bytes 9633792 | tf_op jit(solution)/shard_map/dot_general | solution.py:733
  257.8 2.8 convolution_convert_fusion.7.refs_1_
  262.3 30.3 %attend_back.1 = (bf16[1152,2304]{1,0:T(8,128)(2,1)S(1)}, f32[6,8,1024]{2,1,0:T(8,128)S(1)}) custom-call(bf16[1152,2304]{1,0:T(8,128)(2,1)S(1)} %bitcast.54, bf16[1152,768]{1,0:T(8,128)(2,1)S(1)} %convolution_convert_fusion.5.do_ref, f32[6,8,1152]{2,1,0:T(8,128)S(1)} %get-tuple-element.44.lse_ref, f32[12,128,896]{2,1,0:T(8,128)} %copy-done.3, ...), custom_call_target="tpu_custom_call" | custom-call | tf_op jit(solution)/shard_map/attend_back/pallas_call | solution.py:549
  292.7 5.0 %fusion.17 = (bf16[768]{0:T(1024)(128)(2,1)S(1)}, f32[1152]{0:T(1024)S(1)}, f32[1152,768]{1,0:T(8,128)S(1)}) fusion(f32[1152]{0:T(1024)S(1)} %add_rsqrt_fusion.2, bf16[128,768]{1,0:T(8,128)(2,1)S(1)} %bitcast.66, bf16[1024,768]{1,0:T(8,128)(2,1)S(1)} %bitcast.59, f32[768]{0:T(1024)S(1)} %get-tuple-element.108, ...), kind=kOutput, calls=%fused_computation.31 | convolution fusion | flops 4085708800 | bytes 14169600 | tf_op jit(solution)/shard_map/dot_general | solution.py:739
  297.7 6.8 %convolution_convert_fusion.1.refs_0_ = bf16[768,2304]{1,0:T(8,128)(2,1)} fusion(bf16[1152,2304]{1,0:T(8,128)(2,1)S(1)} %get-tuple-element.46, f32[768]{0:T(1024)S(1)} %get-tuple-element.108, f32[1152]{0:T(1024)S(1)} %add_rsqrt_fusion.2, bf16[128,768]{1,0:T(8,128)(2,1)S(1)} %bitcast.67, bf16[1024,768]{1,0:T(8,128)(2,1)S(1)} %bitcast.60), kind=kOutput, calls=%fused_computation.18 | convolution fusion | flops 4084826112 | bytes 10624512 | tf_op jit(solution)/shard_map/dot_general | solution.py:733
  304.6 3.1 fusion.13
  311.6 123.0 %reduce_grads.1 = (f32[24,2304]{1,0:T(8,128)S(1)}, f32[24,768]{1,0:T(8,128)S(1)}, f32[24,256]{1,0:T(8,128)S(1)}, f32[24,2048]{1,0:T(8,128)S(1)}, f32[24,2048]{1,...) custom-call(bf16[768,2304]{1,0:T(8,128)(2,1)} %convolution_convert_fusion.1.refs_0_, ...), custom_call_target="tpu_custom_call" | custom-call | tf_op jit(solution)/shard_map/reduce_grads/pallas_call | solution.py:400
  440.8 1.8 slice.70
  442.6 3.8 slice.69
  (166 shorter events, 36.3 us)
Async XLA Ops:
  0.6 10.1 %copy-start = (bf16[32,12]{0,1:T(8,128)(2,1)S(1)}, bf16[32,12]{0,1:T(8,128)(2,1)}, u32[]{:S(2)}) copy-start(bf16[32,12]{0,1:T(8,128)(2,1)} %param.33) | copy-start | bytes 2308
  0.7 11.3 %copy-start.11 = (bf16[64,768]{1,0:T(8,128)(2,1)S(1)}, bf16[64,768]{1,0:T(8,128)(2,1)}, u32[]{:S(2)}) copy-start(bf16[64,768]{1,0:T(8,128)(2,1)} %refs_5_.1) | copy-start | bytes 294916
  0.7 11.2 %copy-start.39 = (bf16[24,2048]{1,0:T(8,128)(2,1)S(1)}, bf16[24,2048]{1,0:T(8,128)(2,1)}, u32[]{:S(2)}) copy-start(bf16[24,2048]{1,0:T(8,128)(2,1)} %param.27) | copy-start | bytes 294916
  0.7 11.1 %copy-start.38 = (bf16[24,2048]{1,0:T(8,128)(2,1)S(1)}, bf16[24,2048]{1,0:T(8,128)(2,1)}, u32[]{:S(2)}) copy-start(bf16[24,2048]{1,0:T(8,128)(2,1)} %param.26) | copy-start | bytes 294916
  0.7 112.2 %copy-start.36 = (bf16[2,2,32,768]{3,2,1,0:T(8,128)(2,1)S(1)}, bf16[2,2,32,768]{3,2,1,0:T(8,128)(2,1)}, u32[]{:S(2)}) copy-start(bf16[2,2,32,768]{3,2,1,0:T(8,128)(2,1)} %param.18) | copy-start | bytes 589828
  0.7 112.2 %copy-start.32 = (bf16[2,1,512,768]{3,2,1,0:T(8,128)(2,1)S(1)}, bf16[2,1,512,768]{3,2,1,0:T(8,128)(2,1)}, u32[]{:S(2)}) copy-start(bf16[2,1,512,768]{3,2,1,0:T(8,128)(2,1)} %param.17) | copy-start | bytes 4718596
  111.1 34.1 %copy-start.23 = (bf16[768,768]{1,0:T(8,128)(2,1)}, bf16[768,768]{1,0:T(8,128)(2,1)S(1)}, u32[]{:S(2)}) copy-start(bf16[768,768]{1,0:T(8,128)(2,1)S(1)} %get-tuple-element.38) | copy-start | bytes 3538948
  111.1 37.4 %copy-start.16 = (bf16[768,2048]{1,0:T(8,128)(2,1)}, bf16[768,2048]{1,0:T(8,128)(2,1)S(1)}, u32[]{:S(2)}) copy-start(bf16[768,2048]{1,0:T(8,128)(2,1)S(1)} %get-tuple-element.39) | copy-start | bytes 9437188
  111.1 45.1 %copy-start.14 = (bf16[768,2048]{1,0:T(8,128)(2,1)}, bf16[768,2048]{1,0:T(8,128)(2,1)S(1)}, u32[]{:S(2)}) copy-start(bf16[768,2048]{1,0:T(8,128)(2,1)S(1)} %get-tuple-element.40) | copy-start | bytes 9437188
  118.3 28.7 %copy-start.2 = (bf16[1152,2304]{1,0:T(8,128)(2,1)}, bf16[1152,2304]{1,0:T(8,128)(2,1)S(1)}, u32[]{:S(2)}) copy-start(bf16[1152,2304]{1,0:T(8,128)(2,1)S(1)} %convolution_convert_fusion.qkv_ref) | copy-start | bytes 15925252
  149.9 94.4 %copy-start.34 = (bf16[1152,768]{1,0:T(8,128)(2,1)}, bf16[1152,768]{1,0:T(8,128)(2,1)S(1)}, u32[]{:S(2)}) copy-start(bf16[1152,768]{1,0:T(8,128)(2,1)S(1)} %multiply_convert_fusion.3) | copy-start | bytes 5308420
  156.2 10.6 %copy-start.19 = (bf16[2048,768]{1,0:T(8,128)(2,1)S(1)}, bf16[2048,768]{1,0:T(8,128)(2,1)}, u32[]{:S(2)}) copy-start(bf16[2048,768]{1,0:T(8,128)(2,1)} %copy-done.18) | copy-start | bytes 9437188
  156.2 10.6 %copy-start.30 = (f32[1152,768]{1,0:T(8,128)S(1)}, f32[1152,768]{1,0:T(8,128)}, u32[]{:S(2)}) copy-start(f32[1152,768]{1,0:T(8,128)} %copy-done.29) | copy-start | bytes 10616836
  170.9 32.3 %copy-start.25 = (f32[1152,768]{1,0:T(8,128)}, f32[1152,768]{1,0:T(8,128)S(1)}, u32[]{:S(2)}) copy-start(f32[1152,768]{1,0:T(8,128)S(1)} %get-tuple-element.122) | copy-start | bytes 10616836
  210.8 16.1 %copy-start.27 = (f32[1152,768]{1,0:T(8,128)}, f32[1152,768]{1,0:T(8,128)S(1)}, u32[]{:S(2)}) copy-start(f32[1152,768]{1,0:T(8,128)S(1)} %multiply_subtract_fusion) | copy-start | bytes 10616836
  227.0 8.6 %copy-start.17 = (bf16[768,2048]{1,0:T(8,128)(2,1)S(1)}, bf16[768,2048]{1,0:T(8,128)(2,1)}, u32[]{:S(2)}) copy-start(bf16[768,2048]{1,0:T(8,128)(2,1)} %copy-done.16) | copy-start | bytes 9437188
  227.0 8.6 %copy-start.40 = (bf16[1152,2048]{1,0:T(8,128)(2,1)S(1)}, bf16[1152,2048]{1,0:T(8,128)(2,1)}, u32[]{:S(2)}) copy-start(bf16[1152,2048]{1,0:T(8,128)(2,1)} %get-tuple-element.116) | copy-start | bytes 14155780
  227.0 12.6 %slice-start.2 = ((s8[4718592]{0:T(1024)(128)(4,1)}), s8[4194304]{0:T(1024)(128)(4,1)S(1)}, s32[]{:S(2)}) async-start(s8[4718592]{0:T(1024)(128)(4,1)} %bitcast.78), calls=%async_computation.2 | async-start | bytes 8388608
  250.0 6.2 %copy-start.28 = (f32[1152,768]{1,0:T(8,128)S(1)}, f32[1152,768]{1,0:T(8,128)}, u32[]{:S(2)}) copy-start(f32[1152,768]{1,0:T(8,128)} %copy-done.27) | copy-start | bytes 10616836
  262.2 30.4 %copy-start.13 = (bf16[768,2304]{1,0:T(8,128)(2,1)S(1)}, bf16[768,2304]{1,0:T(8,128)(2,1)}, u32[]{:S(2)}) copy-start(bf16[768,2304]{1,0:T(8,128)(2,1)} %copy-done.12) | copy-start | bytes 10616836
  262.3 30.4 %copy-start.33 = (bf16[2,1,512,768]{3,2,1,0:T(8,128)(2,1)S(1)}, bf16[2,1,512,768]{3,2,1,0:T(8,128)(2,1)}, u32[]{:S(2)}) copy-start(bf16[2,1,512,768]{3,2,1,0:T(8,128)(2,1)} %param.17) | copy-start | bytes 4718596
  262.3 30.4 %copy-start.37 = (bf16[2,2,32,768]{3,2,1,0:T(8,128)(2,1)S(1)}, bf16[2,2,32,768]{3,2,1,0:T(8,128)(2,1)}, u32[]{:S(2)}) copy-start(bf16[2,2,32,768]{3,2,1,0:T(8,128)(2,1)} %param.18) | copy-start | bytes 589828
  440.8 6.3 %copy-start.10 = (f32[24,2048]{1,0:T(8,128)S(1)}, f32[24,2048]{1,0:T(8,128)}, u32[]{:S(2)}) copy-start(f32[24,2048]{1,0:T(8,128)} %copy-done.9) | copy-start | bytes 589828
  440.8 8.3 %copy-start.1 = (bf16[32,12]{0,1:T(8,128)(2,1)S(1)}, bf16[32,12]{0,1:T(8,128)(2,1)}, u32[]{:S(2)}) copy-start(bf16[32,12]{0,1:T(8,128)(2,1)} %param.33) | copy-start | bytes 2308
  (22 other events, 66.2 us)
